TPU v7x, 32 devices: a whole 2x2x4 slice. The times are simulated.
32 devices in a mesh: kv: 2 (over y), blk: 16 (over z, x, core).
Axes of the slice: x: 2, y: 2, z: 4, core: 2. Of those that a mesh axis runs over, the one named last changes fastest.
Arguments:
- suffix_query: bfloat16 [3072, 4096], P('blk', 'kv'), may hold values from -6 to 6
- suffix_key_value: bfloat16 [2, 3072, 2048], P(None, 'blk', 'kv'), may hold values from -6 to 6
- suffix_resid: bfloat16 [3072, 4608], P('blk', 'kv'), may hold values from -6 to 6
- decode_query_rows: bfloat16 [32, 4096], P('blk', 'kv'), may hold values from -6 to 6
- decode_key_value: bfloat16 [2, 32, 2048], P(None, 'blk', 'kv'), may hold values from -6 to 6
- decode_resid: bfloat16 [32, 4608], P('blk', 'kv'), may hold values from -6 to 6
- out_weight: bfloat16 [4096, 4608], P('kv'), may hold values from -1.125 to 1.125
- post_gain: float32 [4608], P('kv'), may hold values from 0.1 to 1.9
- prefix_page_store: bfloat16 [2, 96, 128, 2048], P(None, 'blk', None, 'kv'), may hold values from -6 to 6
- prefix_table: int32 [96], replicated, may hold values from 0 to 95, each once
- decode_page_store: bfloat16 [2, 256, 128, 2048], P(None, 'blk', None, 'kv'), may hold values from -6 to 6
- page_table: int32 [256], replicated, may hold values from 0 to 255, each once
- suffix_lengths: int32 [16], replicated, may hold values from 1 to 768, 3072 in all
- suffix_prefix: int32 [16], replicated, may hold values from 0 to 3
- decode_ages: int32 [32], replicated, may hold values from 1 to 1023, as said below
Outputs:
- suffix_hidden: bfloat16 [3072, 4608], P('blk', 'kv')
- decode_hidden: bfloat16 [32, 4608], P('blk', 'kv')
- new_cache: bfloat16 [2, 256, 128, 2048], P(None, 'blk', None, 'kv')
Inputs may be any that keep to these rules, and one draw needn't show every extreme that they name: `page_table`: every page of the decode pool is named once. `prefix_table`: every page of the prefix pool is named once. `suffix_lengths`: the lengths sum to 3072; one is exactly 768. `decode_ages`: some slot has age 1024 - 1.
All inputs are finite; a program needn't handle non-finite values.
Results may differ from a plain program's by a relative error of at most 0.024.
Values may be sent and summed in bfloat16 or wider, within the bound.
A program may use at most 256 MiB of HBM per device.

v0:
```python
import math

import jax
import jax.numpy as jnp
from jax import lax
from jax.sharding import PartitionSpec as P

D = 4608
QUERY_HEADS = 32
HEAD_SIZE = 128
PAGE_TOKENS = 128
PREFIX_LENGTH = 3072
SLOT_CAPACITY = 1024


soft_cap = 50.0
norm_eps = 1e-06


def from_behind(block, axis, distance):
    devices = range(lax.axis_size(axis))
    route = [(i - distance, i) for i in devices if i - distance in devices]
    return lax.ppermute(block, axis, route)


def attend(query_rows, key_rows, value_rows, visible, q_scale):
    logits = (
        jnp.einsum("qhgd,khd->qhgk", query_rows, key_rows, preferred_element_type=jnp.float32)
        * q_scale
    )
    capped = soft_cap * jnp.tanh(logits / soft_cap)
    weights = jnp.where(visible[:, None, None, :], jnp.exp(capped), 0.0)
    denominator = jnp.sum(weights, axis=3)
    numerator = jnp.einsum(
        "qhgk,khd->qhgd",
        weights.astype(jnp.bfloat16),
        value_rows,
        preferred_element_type=jnp.float32,
    )
    return (numerator, denominator)


def earlier(block_rows):
    return from_behind(block_rows, "blk", 1)


def token_tables(lengths, prefix_ids, token_ids):
    suffix_ends = jnp.cumsum(lengths)
    starts = suffix_ends - lengths
    inside = (
        (token_ids[:, None] >= starts[None, :]) & (token_ids[:, None] < suffix_ends[None, :])
    ).astype(jnp.int32)
    tok_start = jnp.sum(inside * starts[None, :], axis=1)
    tok_prefix = jnp.sum(inside * prefix_ids[None, :], axis=1)
    return (tok_start, tok_prefix)


def inverse_rows(table, wanted):
    hits = (table[None, :] == wanted[:, None]).astype(jnp.int32)
    places = jnp.arange(table.shape[0], dtype=jnp.int32)
    return jnp.sum(hits * places[None, :], axis=1)


def body(
    suffix_query,
    suffix_key_value,
    suffix_resid,
    decode_query_rows,
    decode_key_value,
    decode_resid,
    out_weight,
    post_gain,
    prefix_page_store,
    prefix_table,
    decode_page_store,
    page_table,
    suffix_lengths,
    suffix_prefix,
    decode_ages,
):
    head_dim = HEAD_SIZE
    page_len = PAGE_TOKENS
    q_scale = (D // QUERY_HEADS) ** (-0.5)
    tok_rows = suffix_query.shape[0]
    q_heads = suffix_query.shape[1] // head_dim
    kv_heads = suffix_key_value.shape[2] // head_dim
    query_group_width = q_heads // kv_heads
    my_index = lax.axis_index("blk")
    own_queries = suffix_query.reshape(tok_rows, kv_heads, query_group_width, head_dim)
    token_ids = my_index * tok_rows + jnp.arange(tok_rows, dtype=jnp.int32)
    tok_start, tok_prefix = token_tables(suffix_lengths, suffix_prefix, token_ids)
    look_back = 4
    pieces_back = [suffix_key_value]
    for step in range(look_back):
        pieces_back.insert(0, earlier(pieces_back[0]))
    window = jnp.concatenate(pieces_back, axis=1)
    key_ids = (my_index - look_back) * tok_rows + jnp.arange(
        (look_back + 1) * tok_rows, dtype=jnp.int32
    )
    visible = (key_ids[None, :] >= tok_start[:, None]) & (key_ids[None, :] <= token_ids[:, None])
    window_keys = window[0].reshape((look_back + 1) * tok_rows, kv_heads, head_dim)
    window_values = window[1].reshape((look_back + 1) * tok_rows, kv_heads, head_dim)
    own_numer, own_denom = attend(own_queries, window_keys, window_values, visible, q_scale)
    pool_pages = prefix_table.shape[0]
    page_owner = inverse_rows(prefix_table, jnp.arange(pool_pages, dtype=jnp.int32)) // (
        PREFIX_LENGTH // PAGE_TOKENS
    )
    all_queries = lax.all_gather(suffix_query, "blk", axis=0, tiled=True)
    all_tokens = all_queries.shape[0]
    all_ids = jnp.arange(all_tokens, dtype=jnp.int32)
    unused_start, all_prefix = token_tables(suffix_lengths, suffix_prefix, all_ids)
    local_pages = prefix_page_store.shape[1]
    held_owner = lax.dynamic_slice_in_dim(page_owner, my_index * local_pages, local_pages, 0)
    held_cols = jnp.repeat(held_owner, page_len)
    held_keys = prefix_page_store[0].reshape(local_pages * page_len, kv_heads, head_dim)
    held_values = prefix_page_store[1].reshape(local_pages * page_len, kv_heads, head_dim)
    block_rows = math.gcd(all_tokens, 1024)
    query_blocks = all_queries.reshape(
        all_tokens // block_rows, block_rows, kv_heads, query_group_width, head_dim
    )
    prefix_blocks = all_prefix.reshape(all_tokens // block_rows, block_rows)

    def one_block(element):
        block_queries, block_prefix = element
        seen = block_prefix[:, None] == held_cols[None, :]
        return attend(block_queries, held_keys, held_values, seen, q_scale)

    numer_all, denom_all = lax.map(one_block, (query_blocks, prefix_blocks))
    numer_all = numer_all.reshape(all_tokens, kv_heads, query_group_width, head_dim)
    denom_all = denom_all.reshape(all_tokens, kv_heads, query_group_width)
    pre_numer, pre_denom = (
        lax.psum_scatter(
            numer_all.astype(jnp.bfloat16), "blk", scatter_dimension=0, tiled=True
        ).astype(jnp.float32),
        lax.psum_scatter(
            denom_all.astype(jnp.bfloat16), "blk", scatter_dimension=0, tiled=True
        ).astype(jnp.float32),
    )
    suffix_attn = ((own_numer + pre_numer) / (own_denom + pre_denom)[..., None]).astype(
        jnp.bfloat16
    )
    suffix_attn = suffix_attn.reshape(tok_rows, q_heads * head_dim)
    all_dq, all_dkv = (
        lax.all_gather(decode_query_rows, "blk", axis=0, tiled=True),
        lax.all_gather(decode_key_value, "blk", axis=1, tiled=True),
    )
    slot_total = all_dq.shape[0]
    slot_pages = SLOT_CAPACITY // PAGE_TOKENS
    local_cache = decode_page_store.shape[1]
    page_ids = my_index * local_cache + jnp.arange(local_cache, dtype=jnp.int32)
    position = inverse_rows(page_table, page_ids)
    slot_of = position // slot_pages
    block_of = position % slot_pages
    slot_hot = slot_of[:, None] == jnp.arange(slot_total, dtype=jnp.int32)[None, :]
    page_age = jnp.sum(slot_hot.astype(jnp.int32) * decode_ages[None, :], axis=1)
    select = slot_hot.astype(jnp.bfloat16)
    new_rows = jnp.einsum(
        "ls,tsc->tlc", select, all_dkv, preferred_element_type=jnp.float32
    ).astype(jnp.bfloat16)
    write_here = (block_of == page_age // page_len)[:, None] & (
        jnp.arange(page_len, dtype=jnp.int32)[None, :] == (page_age % page_len)[:, None]
    )
    new_cache = jnp.where(write_here[None, :, :, None], new_rows[:, :, None, :], decode_page_store)
    page_queries = jnp.dot(select, all_dq, preferred_element_type=jnp.float32).astype(jnp.bfloat16)
    page_queries = page_queries.reshape(local_cache, kv_heads, query_group_width, head_dim)
    key_cache = new_cache[0].reshape(local_cache, page_len, kv_heads, head_dim)
    value_cache = new_cache[1].reshape(local_cache, page_len, kv_heads, head_dim)
    logits = (
        jnp.einsum("lhgd,lphd->lhgp", page_queries, key_cache, preferred_element_type=jnp.float32)
        * q_scale
    )
    capped = soft_cap * jnp.tanh(logits / soft_cap)
    places = block_of[:, None] * page_len + jnp.arange(page_len, dtype=jnp.int32)[None, :]
    seen_pos = places <= page_age[:, None]
    weights = jnp.where(seen_pos[:, None, None, :], jnp.exp(capped), 0.0)
    page_denom = jnp.sum(weights, axis=3)
    page_numer = jnp.einsum(
        "lhgp,lphd->lhgd",
        weights.astype(jnp.bfloat16),
        value_cache,
        preferred_element_type=jnp.float32,
    )
    slot_float = slot_hot.astype(jnp.float32)
    slot_numer = jnp.einsum(
        "ls,lhgd->shgd", slot_float, page_numer, precision=lax.Precision.HIGHEST
    )
    slot_denom = jnp.einsum("ls,lhg->shg", slot_float, page_denom, precision=lax.Precision.HIGHEST)
    mine_numer, mine_denom = (
        lax.psum_scatter(
            slot_numer.astype(jnp.bfloat16), "blk", scatter_dimension=0, tiled=True
        ).astype(jnp.float32),
        lax.psum_scatter(
            slot_denom.astype(jnp.bfloat16), "blk", scatter_dimension=0, tiled=True
        ).astype(jnp.float32),
    )
    decode_attn = (mine_numer / mine_denom[..., None]).astype(jnp.bfloat16)
    decode_rows = decode_attn.shape[0]
    decode_attn = decode_attn.reshape(decode_rows, q_heads * head_dim)
    attention = jnp.concatenate([suffix_attn, decode_attn], axis=0)
    projected = jnp.dot(attention, out_weight, preferred_element_type=jnp.float32)
    residual = jnp.concatenate([suffix_resid, decode_resid], axis=0).astype(jnp.float32)
    mine = lax.psum_scatter(
        projected.astype(jnp.bfloat16), "kv", scatter_dimension=1, tiled=True
    ).astype(jnp.float32)
    mean_square = lax.psum(jnp.sum(mine * mine, axis=1), "kv") / D
    normed = mine * lax.rsqrt(mean_square + norm_eps)[:, None] * post_gain[None, :]
    hidden = (residual + normed).astype(jnp.bfloat16)
    return (hidden[:tok_rows], hidden[tok_rows:], new_cache)


def solution(mesh):
    placed = (
        P("blk", "kv"),
        P(None, "blk", "kv"),
        P("blk", "kv"),
        P("blk", "kv"),
        P(None, "blk", "kv"),
        P("blk", "kv"),
        P("kv", None),
        P("kv"),
        P(None, "blk", None, "kv"),
        P(),
        P(None, "blk", None, "kv"),
        P(),
        P(),
        P(),
        P(),
    )
    return jax.shard_map(
        body,
        mesh=mesh,
        in_specs=placed,
        out_specs=(P("blk", "kv"), P("blk", "kv"), P(None, "blk", None, "kv")),
        check_vma=False,
    )
```

profile of v0, /device:TPU:0, one launch (start us, length us, event | category | flops | bytes accessed | tf_op | source)
XLA Modules:
  0.0 570.9 jit_solution(3559114590914880646)
XLA Ops:
  7.2 0.7 all-gather.3.cloned.1.call-update
  7.9 0.7 copy.120
  8.7 11.8 %copy.122 = bf16[2,16,128,1024]{2,3,1,0:T(8,128)(2,1)} copy(bf16[2,16,128,1024]{3,2,1,0:T(8,128)(2,1)} %param.27) | data formatting | bytes 16777216 | tf_op args[10]
  20.5 24.4 %all-gather = bf16[16,2,2048]{2,1,0:T(2,128)(2,1)S(1)} all-gather(bf16[1,2,2048]{2,1,0:T(2,128)(2,1)S(1)} %bitcast.130), channel_id=1, replica_groups=mesh['kv'=2,'blk'=16] {'blk'}, dimensions={0}, use_global_device_ids=true | all-gather | bytes 139264 | tf_op jit(solution)/shard_map/all_gather | solution.py:144
  45.5 18.1 %all_gather.11 = bf16[2,32,1024]{2,0,1:T(2,128)(2,1)S(1)} all-gather(bf16[2,2,1024]{2,0,1:T(2,128)(2,1)S(1)} %copy.120), channel_id=1, replica_groups=mesh['kv'=2,'blk'=16] {'blk'}, dimensions={1}, use_global_device_ids=true | all-gather | bytes 139264 | tf_op jit(solution)/shard_map/all_gather | solution.py:145
  64.2 6.4 %broadcast_select_fusion = bf16[2,16,128,1024]{2,3,1,0:T(8,128)(2,1)S(1)} fusion(bf16[2,16,128,1024]{2,3,1,0:T(8,128)(2,1)} %copy.122, pred[16,128]{1,0:T(8,128)(4,1)S(1)} %fusion.47, bf16[2,16,1024]{2,1,0:T(8,128)(2,1)S(1)} %fusion.32), kind=kLoop, calls=%fused_computation.22 | loop fusion | flops 4194304 | bytes 16844800 | tf_op jit(solution)/shard_map/jit(_where)/select_n | solution.py:163
  70.6 0.8 fusion.58
  71.4 2.5 copy-done
  73.9 1.9 fusion.60
  75.8 2.3 fusion.40
  78.5 0.7 copy.126
  79.7 0.6 copy-done.12
  80.3 0.5 copy-done.14
  81.9 0.4 copy.153
  82.3 1.4 copy.114
  83.8 31.0 %all-gather.3.cloned.1.call-done = bf16[3072,2048]{1,0:T(8,128)(2,1)} async-done(((bf16[192,2048]{1,0:T(8,128)(2,1)}), bf16[3072,2048]{1,0:T(8,128)(2,1)}) %all-gather.3.cloned.1.call-update) | async-done | bytes 12582928 | tf_op jit(solution)/shard_map/all_gather | solution.py:108
  114.8 20.8 %reshape.292 = bf16[3,1024,8,2,128]{4,3,2,1,0:T(2,128)(2,1)} reshape(bf16[3072,2048]{1,0:T(8,128)(2,1)} %all-gather.3.cloned.1.call-done) | data formatting | bytes 25165824 | tf_op jit(solution)/shard_map/reshape | solution.py:118
  135.6 165.5 %while.15 = (s32[]{:T(128)}, bf16[3,1024,8,2,128]{4,1,3,2,0:T(8,128)(2,1)}, bf16[3,1024,8,2]{1,3,2,0:T(2,128)(2,1)S(1)}, s32[3,1024]{1,0:T(4,128)S(1)}, bf16[3,1...) while((s32[]{:T(128)}, ...), condition=%wide.region_6.7_spmd.clone, body=%wide.region_4.6_spmd.clone.sunk | while | flops 6543884288 | bytes 127257216 | solution.py:128
  135.7 0.5 broadcast_compare_fusion.2
  136.2 7.1 %constant_dynamic-slice_fusion.5 = bf16[1,1024,8,2,128]{4,3,2,1,0:T(2,128)(2,1)} fusion(bf16[3,1024,8,2,128]{4,3,2,1,0:T(2,128)(2,1)} %get-tuple-element.288, s32[]{:T(128)} %get-tuple-element.275), kind=kLoop, calls=%fused_computation.14.clone.1 | loop fusion | bytes 8388612 | tf_op jit(solution)/shard_map/while/body/jit(dynamic_index_in_dim)/dynamic_slice | solution.py:128
  143.3 24.4 %bitcast_reduce_fusion.2 = (bf16[1024,8,2]{0,2,1:T(2,128)(2,1)S(1)}, f32[8,1024,2,768]{1,3,2,0:T(8,128)}) fusion(pred[1024,768]{0,1:T(8,128)(4,1)S(1)} %broadcast_compare_fusion.2, bf16[768,8,128]{2,0,1:T(8,128)(2,1)S(1)} %get-tuple-element.289, bf16[1,1024,8,2,128]{4,3,2,1,0:T(2,128)(2,1)} %constant_dynamic-slice_fusion.5), kind=kOutput, calls=%fused_computation.1.clone.1 | convolution fusion | flops 3271540736 | bytes 56918016 | tf_op jit(solution)/shard_map/while/body/eval_jaxpr/qhgd,khd->qhgk/dot_general | solution.py:28
  167.7 23.1 %bitcast_dynamic-update-slice_fusion.4 = bf16[3,1024,8,2,128]{4,1,3,2,0:T(8,128)(2,1)} fusion(bf16[3,1024,8,2,128]{4,1,3,2,0:T(8,128)(2,1)} %get-tuple-element.276, s32[]{:T(128)} %get-tuple-element.275, f32[8,1024,2,768]{1,3,2,0:T(8,128)} %get-tuple-element.264, pred[1024,768]{0,1:T(8,128)(4,1)S(1)} %broadcast_compare_fusion.2, ...), kind=kOutput, calls=%fused_computation.6.clone.1 | convolution fusion | flops 3271557120 | bytes 61080064 | tf_op jit(solution)/shard_map/while/body/eval_jaxpr/qhgk,khd->qhgd/dot_general | solution.py:34
  190.8 0.5 broadcast_compare_fusion.2
  191.4 7.1 %constant_dynamic-slice_fusion.5 = bf16[1,1024,8,2,128]{4,3,2,1,0:T(2,128)(2,1)} fusion(bf16[3,1024,8,2,128]{4,3,2,1,0:T(2,128)(2,1)} %get-tuple-element.288, s32[]{:T(128)} %get-tuple-element.275), kind=kLoop, calls=%fused_computation.14.clone.1 | loop fusion | bytes 8388612 | tf_op jit(solution)/shard_map/while/body/jit(dynamic_index_in_dim)/dynamic_slice | solution.py:128
  198.4 24.3 %bitcast_reduce_fusion.2 = (bf16[1024,8,2]{0,2,1:T(2,128)(2,1)S(1)}, f32[8,1024,2,768]{1,3,2,0:T(8,128)}) fusion(pred[1024,768]{0,1:T(8,128)(4,1)S(1)} %broadcast_compare_fusion.2, bf16[768,8,128]{2,0,1:T(8,128)(2,1)S(1)} %get-tuple-element.289, bf16[1,1024,8,2,128]{4,3,2,1,0:T(2,128)(2,1)} %constant_dynamic-slice_fusion.5), kind=kOutput, calls=%fused_computation.1.clone.1 | convolution fusion | flops 3271540736 | bytes 56918016 | tf_op jit(solution)/shard_map/while/body/eval_jaxpr/qhgd,khd->qhgk/dot_general | solution.py:28
  222.8 23.0 %bitcast_dynamic-update-slice_fusion.4 = bf16[3,1024,8,2,128]{4,1,3,2,0:T(8,128)(2,1)} fusion(bf16[3,1024,8,2,128]{4,1,3,2,0:T(8,128)(2,1)} %get-tuple-element.276, s32[]{:T(128)} %get-tuple-element.275, f32[8,1024,2,768]{1,3,2,0:T(8,128)} %get-tuple-element.264, pred[1024,768]{0,1:T(8,128)(4,1)S(1)} %broadcast_compare_fusion.2, ...), kind=kOutput, calls=%fused_computation.6.clone.1 | convolution fusion | flops 3271557120 | bytes 61080064 | tf_op jit(solution)/shard_map/while/body/eval_jaxpr/qhgk,khd->qhgd/dot_general | solution.py:34
  245.9 0.5 broadcast_compare_fusion.2
  246.4 7.1 %constant_dynamic-slice_fusion.5 = bf16[1,1024,8,2,128]{4,3,2,1,0:T(2,128)(2,1)} fusion(bf16[3,1024,8,2,128]{4,3,2,1,0:T(2,128)(2,1)} %get-tuple-element.288, s32[]{:T(128)} %get-tuple-element.275), kind=kLoop, calls=%fused_computation.14.clone.1 | loop fusion | bytes 8388612 | tf_op jit(solution)/shard_map/while/body/jit(dynamic_index_in_dim)/dynamic_slice | solution.py:128
  253.5 24.3 %bitcast_reduce_fusion.2 = (bf16[1024,8,2]{0,2,1:T(2,128)(2,1)S(1)}, f32[8,1024,2,768]{1,3,2,0:T(8,128)}) fusion(pred[1024,768]{0,1:T(8,128)(4,1)S(1)} %broadcast_compare_fusion.2, bf16[768,8,128]{2,0,1:T(8,128)(2,1)S(1)} %get-tuple-element.289, bf16[1,1024,8,2,128]{4,3,2,1,0:T(2,128)(2,1)} %constant_dynamic-slice_fusion.5), kind=kOutput, calls=%fused_computation.1.clone.1 | convolution fusion | flops 3271540736 | bytes 56918016 | tf_op jit(solution)/shard_map/while/body/eval_jaxpr/qhgd,khd->qhgk/dot_general | solution.py:28
  277.8 23.0 %bitcast_dynamic-update-slice_fusion.4 = bf16[3,1024,8,2,128]{4,1,3,2,0:T(8,128)(2,1)} fusion(bf16[3,1024,8,2,128]{4,1,3,2,0:T(8,128)(2,1)} %get-tuple-element.276, s32[]{:T(128)} %get-tuple-element.275, f32[8,1024,2,768]{1,3,2,0:T(8,128)} %get-tuple-element.264, pred[1024,768]{0,1:T(8,128)(4,1)S(1)} %broadcast_compare_fusion.2, ...), kind=kOutput, calls=%fused_computation.6.clone.1 | convolution fusion | flops 3271557120 | bytes 61080064 | tf_op jit(solution)/shard_map/while/body/eval_jaxpr/qhgk,khd->qhgd/dot_general | solution.py:34
  301.1 1.2 copy.147
  302.3 1.5 reshape.304
  303.8 11.1 %copy.115 = bf16[3,1024,8,2,128]{4,1,0,3,2:T(8,128)(2,1)} copy(bf16[3,1024,8,2,128]{4,1,3,2,0:T(8,128)(2,1)} %get-tuple-element.105) | data formatting | bytes 25165824 | tf_op jit(solution)/shard_map/convert_element_type | solution.py:133
  315.1 1.0 copy-done.4
  316.1 2.2 collective-permute-start
  318.3 1.8 collective-permute-done
  320.1 10.4 %collective-permute-start.1 = (bf16[2,192,1024]{2,1,0:T(8,128)(2,1)S(1)}, bf16[2,192,1024]{2,1,0:T(8,128)(2,1)}, u32[]{:S(2)}, u32[]{:S(2)}) collective-permute-start(bf16[2,192,1024]{2,1,0:T(8,128)(2,1)S(1)} %collective-permute-done), channel_id=1, source_target_pairs={{0,1},{1,2},{2,3},{3,4},{4,5},{5,6},{6,7},{7,8},{8,9},{9,10},{10,1... | collective-permute-start | bytes 2359304 | tf_op jit(solution)/shard_map/ppermute | solution.py:23
  330.5 1.1 collective-permute-done.1
  331.6 12.2 %collective-permute-start.2 = (bf16[2,192,1024]{2,1,0:T(8,128)(2,1)}, bf16[2,192,1024]{2,1,0:T(8,128)(2,1)}, u32[]{:S(2)}, u32[]{:S(2)}) collective-permute-start(bf16[2,192,1024]{2,1,0:T(8,128)(2,1)} %collective-permute-done.1), channel_id=1, source_target_pairs={{0,1},{1,2},{2,3},{3,4},{4,5},{5,6},{6,7},{7,8},{8,9},{9,10},{10,1... | collective-permute-start | bytes 2359304 | tf_op jit(solution)/shard_map/ppermute | solution.py:23
  343.8 0.6 reshape.290
  344.5 0.6 dynamic-slice
  346.0 60.3 %all-reduce = bf16[32,8,2]{1,0,2:T(8,128)(2,1)S(1)} all-reduce(bf16[32,8,2]{1,0,2:T(8,128)(2,1)S(1)} %convolution_convert_fusion.4), channel_id=5, replica_groups=mesh['kv'=2,'blk'=16] {'blk'}, use_global_device_ids=true, to_apply=%region_14.15.clone | all-reduce | flops 512 | bytes 2048
  406.3 1.3 collective-permute-start.3
  407.8 0.9 compare_and_fusion
  408.7 0.8 divide_convert_fusion
  409.8 1.2 constant_dynamic-update-slice_fusion.3
  411.0 1.2 constant_dynamic-update-slice_fusion.2
  412.3 0.9 slice_bitcast_fusion.1
  413.2 0.6 copy.151
  413.7 0.6 copy.150
  414.3 7.3 %fusion.10 = (f32[192,8,2]{0,2,1:T(2,128)S(1)}, f32[8,960,192,2]{1,2,3,0:T(8,128)}) fusion(pred[192,960]{1,0:T(8,128)(4,1)S(1)} %copy-done.6, bf16[192,8,2,128]{3,2,1,0:T(2,128)(2,1)S(1)} %reshape.290, bf16[960,8,128,1]{2,1,0,3:T(8,128)(2,1)S(1)} %bitcast.127), kind=kOutput, calls=%fused_computation.20 | convolution fusion | flops 766768128 | bytes 14745600 | tf_op jit(solution)/shard_map/qhgd,khd->qhgk/dot_general | solution.py:28
  421.6 0.9 reshape.305
  422.6 84.0 %reduce-scatter.8.cloned.1.call-done = bf16[192,8,2,128]{3,0,2,1:T(8,128)(2,1)} async-done(((bf16[3072,8,2,128]{3,0,2,1:T(8,128)(2,1)}), bf16[192,8,2,128]{3,0,2,1:T(8,128)(2,1)}) %reduce-scatter.8.cloned.1.call-update) | async-done | bytes 786448 | tf_op jit(solution)/shard_map/reduce_scatter | solution.py:132
  506.6 6.7 %fusion.23 = bf16[192,8,2,128]{3,0,2,1:T(8,128)(2,1)S(1)} fusion(bf16[192,8,2,128]{3,0,2,1:T(8,128)(2,1)} %reduce-scatter.8.cloned.1.call-done, f32[8,960,192,2]{1,2,3,0:T(8,128)} %get-tuple-element.210, pred[192,960]{1,0:T(8,128)(4,1)S(1)} %copy-done.6, bf16[960,8,128,1]{2,1,0,3:T(8,128)(2,1)S(1)} %bitcast.126, f32[192,8,2]{0,2,1:T(2,128)S(1)} %copy.118), kind=kOutput, calls=%fused_computation.40 | convolution fusion | flops 768344064 | bytes 15532032 | tf_op jit(solution)/shard_map/qhgk,khd->qhgd/dot_general | solution.py:34
  513.3 0.8 copy.119
  514.1 0.6 reshape.293
  514.7 11.6 %convolution_convert_fusion = bf16[194,4608]{1,0:T(8,128)(2,1)} fusion(bf16[2048,4608]{1,0:T(8,128)(2,1)} %param.23, bf16[2,2048]{1,0:T(2,128)(2,1)S(1)} %reshape.295, bf16[192,2048]{1,0:T(8,128)(2,1)S(1)} %reshape.293), kind=kOutput, calls=%fused_computation.23 | convolution fusion | flops 3664110592 | bytes 21456896 | tf_op jit(solution)/shard_map/dot_general | solution.py:200
  526.4 11.9 %copy.130 = bf16[2,16,128,1024]{3,2,1,0:T(8,128)(2,1)} copy(bf16[2,16,128,1024]{2,3,1,0:T(8,128)(2,1)} %copy-done) | data formatting | bytes 16777216
  538.3 16.4 %reduce-scatter.12.cloned.1.call-done = bf16[194,2304]{1,0:T(8,128)(2,1)} async-done(((bf16[194,4608]{1,0:T(8,128)(2,1)}), bf16[194,2304]{1,0:T(8,128)(2,1)}) %reduce-scatter.12.cloned.1.call-update) | async-done | bytes 893968 | tf_op jit(solution)/shard_map/reduce_scatter | solution.py:202
  554.7 1.4 fusion.18
  556.2 4.9 psum.7
  561.1 1.6 fusion.21
  562.8 1.0 slice.36
  563.7 0.6 slice.37
  (106 shorter events, 4.7 us)
Async XLA Ops:
  7.2 107.6 %all-gather.3.cloned.1.call-start = ((), (), s32[]{:S(2)}) async-start(), calls=%async_computation.4 | async-start | bytes 13369344 | tf_op jit(solution)/shard_map/all_gather | solution.py:108
  7.9 400.8 %reduce-scatter.10.cloned.1.call-start = ((), (), s32[]{:S(2)}) async-start(), calls=%async_computation.6 | async-start | bytes 139264 | tf_op jit(solution)/shard_map/reduce_scatter | solution.py:189
  8.7 11.9 %copy-start.9 = (bf16[2,2048]{1,0:T(2,128)(2,1)S(1)}, bf16[2,2048]{1,0:T(2,128)(2,1)}, u32[]{:S(2)}) copy-start(bf16[2,2048]{1,0:T(2,128)(2,1)} %param.20) | copy-start | bytes 24580
  8.7 36.3 %copy-start.16 = (s32[256]{0:T(256)S(1)}, s32[256]{0:T(256)}, u32[]{:S(2)}) copy-start(s32[256]{0:T(256)} %param.28) | copy-start | bytes 3076
  8.7 54.9 %copy-start.19 = (s32[32]{0:T(128)S(1)}, s32[32]{0:T(128)}, u32[]{:S(2)}) copy-start(s32[32]{0:T(128)} %param.31) | copy-start | bytes 388
  45.2 32.9 %copy-start.10 = (s32[16]{0:T(128)}, s32[16]{0:T(128)S(1)}, u32[]{:S(2)}) copy-start(s32[16]{0:T(128)S(1)} %and_select_fusion.3) | copy-start | bytes 196
  70.6 3.3 copy-start
  73.9 5.4 copy-start.20
  73.9 5.6 copy-start.18
  73.9 6.9 %copy-start.17 = (s32[16]{0:T(128)S(1)}, s32[16]{0:T(128)}, u32[]{:S(2)}) copy-start(s32[16]{0:T(128)} %param.30) | copy-start | bytes 196
  73.9 7.0 %copy-start.1 = (bf16[2,6,128,1024]{3,2,1,0:T(8,128)(2,1)S(1)}, bf16[2,6,128,1024]{3,2,1,0:T(8,128)(2,1)}, u32[]{:S(2)}) copy-start(bf16[2,6,128,1024]{3,2,1,0:T(8,128)(2,1)} %param.25) | copy-start | bytes 9437188
  79.2 342.4 %reduce-scatter.14.cloned.1.call-start = ((), (), s32[]{:S(2)}) async-start(), calls=%async_computation.8 | async-start | bytes 835584
  79.7 0.6 copy-start.12
  80.3 0.5 copy-start.14
  303.8 202.8 %reduce-scatter.8.cloned.1.call-start = ((), (), s32[]{:S(2)}) async-start(), calls=%async_computation.5 | async-start | bytes 13369344 | tf_op jit(solution)/shard_map/reduce_scatter | solution.py:132
  314.9 1.1 copy-start.4
  314.9 28.8 %copy-start.2 = (bf16[192,2048]{1,0:T(8,128)(2,1)S(1)}, bf16[192,2048]{1,0:T(8,128)(2,1)}, u32[]{:S(2)}) copy-start(bf16[192,2048]{1,0:T(8,128)(2,1)} %param.17) | copy-start | bytes 2359300
  314.9 29.4 %copy-start.5 = (f32[16,8,2]{2,1,0:T(8,128)S(1)}, f32[16,8,2]{2,1,0:T(8,128)}, u32[]{:S(2)}) copy-start(f32[16,8,2]{2,1,0:T(8,128)} %get-tuple-element.207) | copy-start | bytes 3076
  315.0 29.5 %copy-start.21 = (u32[32]{0:T(128)S(1)}, u32[32]{0:T(128)}, u32[]{:S(2)}) copy-start(u32[32]{0:T(128)} %constant.146) | copy-start | bytes 388
  315.0 30.8 %copy-start.11 = (s32[16]{0:T(128)S(1)}, s32[16]{0:T(128)}, u32[]{:S(2)}) copy-start(s32[16]{0:T(128)} %copy-done.10) | copy-start | bytes 196
  315.0 92.7 %copy-start.13 = (s32[16]{0:T(128)S(1)}, s32[16]{0:T(128)}, u32[]{:S(2)}) copy-start(s32[16]{0:T(128)} %copy-done.12) | copy-start | bytes 196
  315.0 92.7 %copy-start.15 = (s32[16]{0:T(128)S(1)}, s32[16]{0:T(128)}, u32[]{:S(2)}) copy-start(s32[16]{0:T(128)} %copy-done.14) | copy-start | bytes 196
  315.0 239.7 %reduce-scatter.12.cloned.1.call-start = ((), (), s32[]{:S(2)}) async-start(), calls=%async_computation.7 | async-start | bytes 2764800 | tf_op jit(solution)/shard_map/reduce_scatter | solution.py:202
  316.1 4.0 collective-permute-start
  320.1 11.5 %collective-permute-start.1 = (bf16[2,192,1024]{2,1,0:T(8,128)(2,1)S(1)}, bf16[2,192,1024]{2,1,0:T(8,128)(2,1)}, u32[]{:S(2)}, u32[]{:S(2)}) collective-permute-start(bf16[2,192,1024]{2,1,0:T(8,128)(2,1)S(1)} %collective-permute-done), channel_id=1, source_target_pairs={{0,1},{1,2},{2,3},{3,4},{4,5},{5,6},{6,7},{7,8},{8,9},{9,10},{10,1... | collective-permute-start | bytes 2359304 | tf_op jit(solution)/shard_map/ppermute | solution.py:23
  331.6 74.7 %collective-permute-start.2 = (bf16[2,192,1024]{2,1,0:T(8,128)(2,1)}, bf16[2,192,1024]{2,1,0:T(8,128)(2,1)}, u32[]{:S(2)}, u32[]{:S(2)}) collective-permute-start(bf16[2,192,1024]{2,1,0:T(8,128)(2,1)} %collective-permute-done.1), channel_id=1, source_target_pairs={{0,1},{1,2},{2,3},{3,4},{4,5},{5,6},{6,7},{7,8},{8,9},{9,10},{10,1... | collective-permute-start | bytes 2359304 | tf_op jit(solution)/shard_map/ppermute | solution.py:23
  406.3 3.4 collective-permute-start.3
  413.2 1.2 copy-start.6
  526.4 34.7 %copy-start.3 = (bf16[192,2304]{1,0:T(8,128)(2,1)S(1)}, bf16[192,2304]{1,0:T(8,128)(2,1)}, u32[]{:S(2)}) copy-start(bf16[192,2304]{1,0:T(8,128)(2,1)} %param.19) | copy-start | bytes 2654212
  526.4 34.7 %copy-start.7 = (f32[2304]{0:T(1024)S(1)}, f32[2304]{0:T(1024)}, u32[]{:S(2)}) copy-start(f32[2304]{0:T(1024)} %param.24) | copy-start | bytes 27652
  526.4 34.7 %copy-start.8 = (bf16[2,2304]{1,0:T(2,128)(2,1)S(1)}, bf16[2,2304]{1,0:T(2,128)(2,1)}, u32[]{:S(2)}) copy-start(bf16[2,2304]{1,0:T(2,128)(2,1)} %param.22) | copy-start | bytes 27652
Sparse Core Ops, SparseCore 0:
  10.3 104.4 all-gather.2
  118.3 53.3 reduce-scatter.9
  303.9 56.4 reduce-scatter.13
  364.8 141.7 reduce-scatter.7
  526.5 28.1 reduce-scatter.11
where the time goes:
time: 573 us; the launch traced here: 571 us
  matrix products  173 us (30%)
  waiting for transfers between devices  135 us (24%)
  blocking collectives  108 us (19%)
  local copies, waits for them, and re-layouts  99.7 us (17%)
  starting transfers between devices  26.3 us (5%)
  between operations  14.9 us (3%)
  other arithmetic  13.8 us (2%)
    reduce_scatter x1, waiting for transfers between devices, body(): lax.psum_scatter(numer_all.astype(jnp.bfloat16), 'blk', scatter_dimension...  84 us
    dot_general x4, matrix products, attend(): jnp.einsum('qhgd,khd->qhgk', query_rows, key_rows, preferred_element_type...  80.3 us
    dot_general x4, matrix products, attend(): jnp.einsum('qhgk,khd->qhgd', weights.astype(jnp.bfloat16), value_rows, pr...  75.8 us
    unnamed x1, blocking collectives  60.3 us
    unnamed x64, local copies, waits for them, and re-layouts  40.4 us
    all_gather x1, waiting for transfers between devices, body(): all_queries = lax.all_gather(suffix_query, 'blk', axis=0, tiled=True)  31 us
    ppermute x4, starting transfers between devices, from_behind(): return lax.ppermute(block, axis, route)  26.1 us
    all_gather x1, blocking collectives, body(): lax.all_gather(decode_query_rows, 'blk', axis=0, tiled=True)  24.4 us
  transfers between devices with their start and end apart: 9, of which 6 were waited for; matrix products, arithmetic and copies ran while one was open for 45% of the time, Pallas kernels for 0%

commit v1 on v0

--- a/solution.py
+++ b/solution.py
@@ -1,8 +1,11 @@
+import functools
 import math
 
 import jax
 import jax.numpy as jnp
 from jax import lax
+from jax.experimental import pallas as pl
+from jax.experimental.pallas import tpu as pltpu
 from jax.sharding import PartitionSpec as P
 
 D = 4608
@@ -15,33 +18,6 @@
 
 soft_cap = 50.0
 norm_eps = 1e-06
-
-
-def from_behind(block, axis, distance):
-    devices = range(lax.axis_size(axis))
-    route = [(i - distance, i) for i in devices if i - distance in devices]
-    return lax.ppermute(block, axis, route)
-
-
-def attend(query_rows, key_rows, value_rows, visible, q_scale):
-    logits = (
-        jnp.einsum("qhgd,khd->qhgk", query_rows, key_rows, preferred_element_type=jnp.float32)
-        * q_scale
-    )
-    capped = soft_cap * jnp.tanh(logits / soft_cap)
-    weights = jnp.where(visible[:, None, None, :], jnp.exp(capped), 0.0)
-    denominator = jnp.sum(weights, axis=3)
-    numerator = jnp.einsum(
-        "qhgk,khd->qhgd",
-        weights.astype(jnp.bfloat16),
-        value_rows,
-        preferred_element_type=jnp.float32,
-    )
-    return (numerator, denominator)
-
-
-def earlier(block_rows):
-    return from_behind(block_rows, "blk", 1)
 
 
 def token_tables(lengths, prefix_ids, token_ids):
@@ -59,6 +35,211 @@
     hits = (table[None, :] == wanted[:, None]).astype(jnp.int32)
     places = jnp.arange(table.shape[0], dtype=jnp.int32)
     return jnp.sum(hits * places[None, :], axis=1)
+
+
+TILE = 128
+
+
+def attention_kernel(
+    order,
+    offsets,
+    flags,
+    low,
+    high,
+    group_base,
+    q_ref,
+    start_ref,
+    prefix_ref,
+    kv_ref,
+    numer_ref,
+    denom_ref,
+    keys,
+    values,
+    own_keys,
+    own_values,
+    acc,
+    wacc,
+    sems,
+    *,
+    prefixes,
+    sources,
+    local_pages,
+    tok_rows,
+    q_scale,
+):
+    page_len = PAGE_TOKENS
+    tile = pl.program_id(0)
+
+    @pl.when(tile == 0)
+    def _():
+        def fetch_page(i, carry):
+            entry = order[i]
+            j = entry // local_pages
+            rows = pl.ds(pl.multiple_of((entry % local_pages) * page_len, page_len), page_len)
+            to = pl.ds(pl.multiple_of(i * page_len, page_len), page_len)
+            pltpu.make_async_copy(kv_ref.at[j, 0, rows], keys.at[to], sems.at[0]).start()
+            pltpu.make_async_copy(kv_ref.at[j, 1, rows], values.at[to], sems.at[1]).start()
+            return carry
+
+        lax.fori_loop(0, sources * local_pages, fetch_page, 0)
+        for j in range(sources):
+            rows = pl.ds(local_pages * page_len, tok_rows)
+            to = pl.ds(j * tok_rows, tok_rows)
+            pltpu.make_async_copy(kv_ref.at[j, 0, rows], own_keys.at[to], sems.at[2]).start()
+            pltpu.make_async_copy(kv_ref.at[j, 1, rows], own_values.at[to], sems.at[3]).start()
+        pltpu.make_async_copy(keys, keys, sems.at[0]).wait()
+        pltpu.make_async_copy(values, values, sems.at[1]).wait()
+        pltpu.make_async_copy(own_keys, own_keys, sems.at[2]).wait()
+        pltpu.make_async_copy(own_values, own_values, sems.at[3]).wait()
+
+    q = q_ref[...]
+    half = HEAD_SIZE
+    rows_q = jnp.concatenate([q[:, :half], q[:, half:]], axis=0)
+    row_prefix = prefix_ref[...]
+    row_prefix = jnp.concatenate([row_prefix, row_prefix], axis=0)
+    row_start = start_ref[...]
+    row_start = jnp.concatenate([row_start, row_start], axis=0)
+    acc[...] = jnp.zeros_like(acc)
+    wacc[...] = jnp.zeros_like(wacc)
+    inner = q_scale / soft_cap
+    outer = soft_cap * math.log2(math.e)
+
+    def weights_of(key_rows):
+        logits = lax.dot_general(
+            rows_q, key_rows, (((1,), (1,)), ((), ())), preferred_element_type=jnp.float32
+        )
+        return jnp.exp2(jnp.tanh(logits * inner) * outer)
+
+    def folded(w):
+        out = w[:, :half]
+        for k in range(1, w.shape[1] // half):
+            out = out + w[:, k * half : (k + 1) * half]
+        return out
+
+    for p in range(prefixes):
+
+        @pl.when(flags[tile * prefixes + p] != 0)
+        def _():
+            first = offsets[p]
+            count = offsets[p + 1] - first
+
+            def step(width):
+                def run(c, carry):
+                    num, den = carry
+                    at = pl.ds(
+                        pl.multiple_of((first + c) * page_len, page_len), width * page_len
+                    )
+                    w = weights_of(keys[at, :])
+                    num = num + jnp.dot(
+                        w.astype(jnp.bfloat16), values[at, :], preferred_element_type=jnp.float32
+                    )
+                    return num, den + folded(w)
+
+                return run
+
+            zero = jnp.zeros((2 * TILE, half), jnp.float32)
+            four = step(4)
+            carry = lax.fori_loop(0, count // 4, lambda c, s: four(4 * c, s), (zero, zero))
+            num, den = lax.fori_loop(count // 4 * 4, count, step(1), carry)
+            mine = row_prefix == p
+            acc[...] += jnp.where(mine, num, 0.0)
+            wacc[...] += jnp.where(mine, den, 0.0)
+
+    row_id = tile * TILE + lax.broadcasted_iota(jnp.int32, (TILE, 1), 0)
+    row_id = jnp.concatenate([row_id, row_id], axis=0)
+
+    def own(c, carry):
+        at = pl.ds(pl.multiple_of(c * TILE, TILE), TILE)
+        key_id = (
+            group_base[0] + c * TILE + lax.broadcasted_iota(jnp.int32, (2 * TILE, TILE), 1)
+        )
+        seen = (key_id >= row_start) & (key_id <= row_id)
+        w = jnp.where(seen, weights_of(own_keys[at, :]), 0.0)
+        acc[...] += jnp.dot(
+            w.astype(jnp.bfloat16), own_values[at, :], preferred_element_type=jnp.float32
+        )
+        wacc[...] += w
+        return carry
+
+    lax.fori_loop(low[tile], high[tile], own, 0)
+    numer_ref[...] = jnp.concatenate([acc[:TILE, :], acc[TILE:, :]], axis=1).astype(
+        numer_ref.dtype
+    )
+    denom_ref[0] = lax.dot_general(
+        jnp.ones((8, half), jnp.float32),
+        wacc[...],
+        (((1,), (1,)), ((), ())),
+        preferred_element_type=jnp.float32,
+        precision=lax.Precision.HIGHEST,
+    )
+
+
+def head_attention(q_all, kv_group, tok_start, tok_prefix, page_owner, base_page, base_token,
+                   prefixes, local_pages, tok_rows, q_scale):
+    tokens, width = q_all.shape
+    sources = kv_group.shape[0]
+    pages = sources * local_pages
+    tiles = tokens // TILE
+    owned = lax.dynamic_slice_in_dim(page_owner, base_page, pages, 0)
+    place = jnp.arange(pages, dtype=jnp.int32)
+    rank = owned * pages + place
+    position = jnp.sum((rank[None, :] < rank[:, None]).astype(jnp.int32), axis=1)
+    order = jnp.sum(
+        (position[None, :] == place[:, None]).astype(jnp.int32) * place[None, :], axis=1
+    )
+    ids = jnp.arange(prefixes + 1, dtype=jnp.int32)
+    offsets = jnp.sum((owned[None, :] < ids[:, None]).astype(jnp.int32), axis=1)
+    tile_prefix = tok_prefix.reshape(tiles, TILE)
+    flags = (
+        jnp.any(tile_prefix[:, :, None] == ids[None, None, :prefixes], axis=1)
+        .astype(jnp.int32)
+        .reshape(-1)
+    )
+    group_tokens = sources * tok_rows
+    tile_first = jnp.arange(tiles, dtype=jnp.int32) * TILE
+    low = jnp.clip(tok_start.reshape(tiles, TILE)[:, 0] - base_token, 0, group_tokens) // TILE
+    high = (jnp.clip(tile_first + TILE - base_token, 0, group_tokens) + TILE - 1) // TILE
+    run = functools.partial(
+        attention_kernel,
+        prefixes=prefixes,
+        sources=sources,
+        local_pages=local_pages,
+        tok_rows=tok_rows,
+        q_scale=q_scale,
+    )
+    return pl.pallas_call(
+        run,
+        out_shape=(
+            jax.ShapeDtypeStruct((tokens, width), jnp.bfloat16),
+            jax.ShapeDtypeStruct((tiles, 8, 2 * TILE), jnp.float32),
+        ),
+        grid_spec=pltpu.PrefetchScalarGridSpec(
+            num_scalar_prefetch=6,
+            grid=(tiles,),
+            in_specs=[
+                pl.BlockSpec((TILE, width), lambda i, *_: (i, 0)),
+                pl.BlockSpec((TILE, 1), lambda i, *_: (i, 0)),
+                pl.BlockSpec((TILE, 1), lambda i, *_: (i, 0)),
+                pl.BlockSpec(memory_space=pl.ANY),
+            ],
+            out_specs=[
+                pl.BlockSpec((TILE, width), lambda i, *_: (i, 0)),
+                pl.BlockSpec((1, 8, 2 * TILE), lambda i, *_: (i, 0, 0)),
+            ],
+            scratch_shapes=[
+                pltpu.VMEM((pages * PAGE_TOKENS, HEAD_SIZE), jnp.bfloat16),
+                pltpu.VMEM((pages * PAGE_TOKENS, HEAD_SIZE), jnp.bfloat16),
+                pltpu.VMEM((group_tokens, HEAD_SIZE), jnp.bfloat16),
+                pltpu.VMEM((group_tokens, HEAD_SIZE), jnp.bfloat16),
+                pltpu.VMEM((2 * TILE, HEAD_SIZE), jnp.float32),
+                pltpu.VMEM((2 * TILE, HEAD_SIZE), jnp.float32),
+                pltpu.SemaphoreType.DMA((4,)),
+            ],
+        ),
+        compiler_params=pltpu.CompilerParams(vmem_limit_bytes=32 * 1024 * 1024),
+        name="head_attention",
+    )(order, offsets, flags, low, high, base_token[None], q_all, tok_start[:, None],
+      tok_prefix[:, None], kv_group)
 
 
 def body(
@@ -86,59 +267,53 @@
     kv_heads = suffix_key_value.shape[2] // head_dim
     query_group_width = q_heads // kv_heads
     my_index = lax.axis_index("blk")
-    own_queries = suffix_query.reshape(tok_rows, kv_heads, query_group_width, head_dim)
-    token_ids = my_index * tok_rows + jnp.arange(tok_rows, dtype=jnp.int32)
-    tok_start, tok_prefix = token_tables(suffix_lengths, suffix_prefix, token_ids)
-    look_back = 4
-    pieces_back = [suffix_key_value]
-    for step in range(look_back):
-        pieces_back.insert(0, earlier(pieces_back[0]))
-    window = jnp.concatenate(pieces_back, axis=1)
-    key_ids = (my_index - look_back) * tok_rows + jnp.arange(
-        (look_back + 1) * tok_rows, dtype=jnp.int32
-    )
-    visible = (key_ids[None, :] >= tok_start[:, None]) & (key_ids[None, :] <= token_ids[:, None])
-    window_keys = window[0].reshape((look_back + 1) * tok_rows, kv_heads, head_dim)
-    window_values = window[1].reshape((look_back + 1) * tok_rows, kv_heads, head_dim)
-    own_numer, own_denom = attend(own_queries, window_keys, window_values, visible, q_scale)
+    blocks = lax.axis_size("blk")
+    groups = blocks // kv_heads
+    group = my_index // kv_heads
+    pair = query_group_width * head_dim
+    all_tokens = blocks * tok_rows
+    all_ids = jnp.arange(all_tokens, dtype=jnp.int32)
+    tok_start, tok_prefix = token_tables(suffix_lengths, suffix_prefix, all_ids)
     pool_pages = prefix_table.shape[0]
-    page_owner = inverse_rows(prefix_table, jnp.arange(pool_pages, dtype=jnp.int32)) // (
-        PREFIX_LENGTH // PAGE_TOKENS
-    )
-    all_queries = lax.all_gather(suffix_query, "blk", axis=0, tiled=True)
-    all_tokens = all_queries.shape[0]
-    all_ids = jnp.arange(all_tokens, dtype=jnp.int32)
-    unused_start, all_prefix = token_tables(suffix_lengths, suffix_prefix, all_ids)
+    per_prefix = PREFIX_LENGTH // PAGE_TOKENS
+    page_owner = (
+        inverse_rows(prefix_table, jnp.arange(pool_pages, dtype=jnp.int32)) // per_prefix
+    )
     local_pages = prefix_page_store.shape[1]
-    held_owner = lax.dynamic_slice_in_dim(page_owner, my_index * local_pages, local_pages, 0)
-    held_cols = jnp.repeat(held_owner, page_len)
-    held_keys = prefix_page_store[0].reshape(local_pages * page_len, kv_heads, head_dim)
-    held_values = prefix_page_store[1].reshape(local_pages * page_len, kv_heads, head_dim)
-    block_rows = math.gcd(all_tokens, 1024)
-    query_blocks = all_queries.reshape(
-        all_tokens // block_rows, block_rows, kv_heads, query_group_width, head_dim
-    )
-    prefix_blocks = all_prefix.reshape(all_tokens // block_rows, block_rows)
-
-    def one_block(element):
-        block_queries, block_prefix = element
-        seen = block_prefix[:, None] == held_cols[None, :]
-        return attend(block_queries, held_keys, held_values, seen, q_scale)
-
-    numer_all, denom_all = lax.map(one_block, (query_blocks, prefix_blocks))
-    numer_all = numer_all.reshape(all_tokens, kv_heads, query_group_width, head_dim)
-    denom_all = denom_all.reshape(all_tokens, kv_heads, query_group_width)
-    pre_numer, pre_denom = (
-        lax.psum_scatter(
-            numer_all.astype(jnp.bfloat16), "blk", scatter_dimension=0, tiled=True
-        ).astype(jnp.float32),
-        lax.psum_scatter(
-            denom_all.astype(jnp.bfloat16), "blk", scatter_dimension=0, tiled=True
-        ).astype(jnp.float32),
-    )
-    suffix_attn = ((own_numer + pre_numer) / (own_denom + pre_denom)[..., None]).astype(
-        jnp.bfloat16
-    )
+    q_send = suffix_query.reshape(tok_rows, kv_heads, pair).transpose(1, 0, 2)
+    q_send = jnp.broadcast_to(q_send[None], (groups,) + q_send.shape)
+    q_send = q_send.reshape(blocks, tok_rows, pair)
+    q_all = lax.all_to_all(q_send, "blk", 0, 0, tiled=True).reshape(all_tokens, pair)
+    kv_send = jnp.concatenate(
+        [prefix_page_store.reshape(2, local_pages * page_len, -1), suffix_key_value], axis=1
+    )
+    kv_send = kv_send.reshape(2, -1, kv_heads, head_dim).transpose(2, 0, 1, 3)
+    members = [[g * kv_heads + h for h in range(kv_heads)] for g in range(groups)]
+    kv_group = lax.all_to_all(
+        kv_send, "blk", 0, 0, tiled=True, axis_index_groups=members
+    )
+    numer, denom = head_attention(
+        q_all,
+        kv_group,
+        tok_start,
+        tok_prefix,
+        page_owner,
+        group * kv_heads * local_pages,
+        group * kv_heads * tok_rows,
+        pool_pages // per_prefix,
+        local_pages,
+        tok_rows,
+        q_scale,
+    )
+    denom = denom[:, 0, :].reshape(-1, query_group_width, TILE).transpose(1, 0, 2)
+    denom = denom.reshape(query_group_width, blocks, tok_rows).transpose(1, 0, 2)
+    numer = lax.all_to_all(numer.reshape(blocks, tok_rows, pair), "blk", 0, 0, tiled=True)
+    denom = lax.all_to_all(denom, "blk", 0, 0, tiled=True)
+    numer = numer.reshape(groups, kv_heads, tok_rows, query_group_width, head_dim)
+    numer = jnp.sum(numer.astype(jnp.float32), axis=0)
+    denom = jnp.sum(denom.reshape(groups, kv_heads, query_group_width, tok_rows), axis=0)
+    suffix_attn = numer / denom.transpose(0, 2, 1)[..., None]
+    suffix_attn = suffix_attn.astype(jnp.bfloat16).transpose(1, 0, 2, 3)
     suffix_attn = suffix_attn.reshape(tok_rows, q_heads * head_dim)
     all_dq, all_dkv = (
         lax.all_gather(decode_query_rows, "blk", axis=0, tiled=True),

time: 573 us -> 401 us (0.70)
  matrix products: 173 us -> 16.3 us
  waiting for transfers between devices: 135 us -> 47.5 us
  Pallas kernels: 0 us -> 81.2 us
  local copies, waits for them, and re-layouts: 99.7 us -> 49.3 us
  blocking collectives: 108 us -> 142 us
  other arithmetic: 13.8 us -> 20 us
    dot_general x8 -> x0, matrix products: 156 us -> none  [the longest x4 80.3 us: attend(): jnp.einsum('qhgd,khd->qhgk', query_rows, key_rows, preferred_element_type...]
    reduce_scatter x1 -> x0, waiting for transfers between devices: 84 us -> none  [body(): lax.psum_scatter(numer_all.astype(jnp.bfloat16), 'blk', scatter_dimension...]
    pallas_call x0 -> x1, Pallas kernels: none -> 81.2 us  [head_attention(): pl.pallas_call(run, out_shape=(jax.ShapeDtypeStruct((tokens, width), jnp....]
    all_to_all x0 -> x4, waiting for transfers between devices: none -> 32.8 us  [the longest x1 26.2 us: body(): lax.all_to_all(q_send, 'blk', 0, 0, tiled=True).reshape(all_tokens, pair)]
    all_gather x1, blocking collectives: 24.4 us -> 56.3 us  [body(): lax.all_gather(decode_query_rows, 'blk', axis=0, tiled=True)]
    all_gather x1 -> x0, waiting for transfers between devices: 31 us -> none  [body(): all_queries = lax.all_gather(suffix_query, 'blk', axis=0, tiled=True)]
    ppermute x4 -> x0, starting transfers between devices: 26.1 us -> none  [from_behind(): return lax.ppermute(block, axis, route)]
    all_to_all x0 -> x4, starting transfers between devices: none -> 25.7 us  [the longest x1 8.16 us: body(): lax.all_to_all(kv_send, 'blk', 0, 0, tiled=True, axis_index_groups=members)]
  transfers between devices with their start and end apart: 9 -> 6, of which waited for: 6 -> 3; matrix products, arithmetic and copies ran while one was open for 45% -> 12% of each run, Pallas kernels for 0% -> 0%
where the time goes in v1:
time: 401 us; the launch traced here: 397 us
  blocking collectives  142 us (35%)
  Pallas kernels  81.2 us (20%)
  local copies, waits for them, and re-layouts  49.3 us (12%)
  waiting for transfers between devices  47.5 us (12%)
  starting transfers between devices  25.8 us (6%)
  other arithmetic  20 us (5%)
  matrix products  16.3 us (4%)
  between operations  15.2 us (4%)
    pallas_call x1, Pallas kernels, head_attention(): pl.pallas_call(run, out_shape=(jax.ShapeDtypeStruct((tokens, width), jnp....  81.2 us
    unnamed x1, blocking collectives  62 us
    all_gather x1, blocking collectives, body(): lax.all_gather(decode_query_rows, 'blk', axis=0, tiled=True)  56.3 us
    unnamed x42, local copies, waits for them, and re-layouts  34.8 us
    all_to_all x1, waiting for transfers between devices, body(): lax.all_to_all(q_send, 'blk', 0, 0, tiled=True).reshape(all_tokens, pair)  26.2 us
    all_gather x1, blocking collectives, body(): lax.all_gather(decode_key_value, 'blk', axis=1, tiled=True)  18.7 us
    reduce_scatter x1, waiting for transfers between devices, body(): lax.psum_scatter(projected.astype(jnp.bfloat16), 'kv', scatter_dimension=...  14.7 us
    dot_general x1, matrix products, body(): jnp.dot(attention, out_weight, preferred_element_type=jnp.float32)  11.7 us
  transfers between devices with their start and end apart: 6, of which 3 were waited for; matrix products, arithmetic and copies ran while one was open for 12% of the time, Pallas kernels for 0%

profile of v1, /device:TPU:0, one launch (start us, length us, event | category | flops | bytes accessed | tf_op | source)
XLA Modules:
  0.0 397.3 jit_solution(3904773086166419204)
XLA Ops:
  7.2 1.4 copy.133
  8.6 0.2 copy.104
  8.7 1.3 broadcast_in_dim.27
  10.1 7.4 %all-to-all-start = ((bf16[16,192,256]{2,1,0:T(8,128)(2,1)}), bf16[16,192,256]{2,1,0:T(8,128)(2,1)S(1)}, u32[]{:S(2)}, u32[]{:S(2)}) async-start(bf16[16,192,256]{2,1,0:T(8,128)(2,1)} %bitcast.70), calls=%async_computation | async-start | bytes 3145728 | tf_op jit(solution)/shard_map/all_to_all | solution.py:286
  17.4 2.7 copy.134
  20.1 0.6 copy.105
  20.8 0.2 copy_bitcast_fusion
  21.0 2.3 maximum_bitcast_fusion
  23.2 26.2 %all-to-all-done = bf16[16,192,256]{2,1,0:T(8,128)(2,1)S(1)} async-done(((bf16[16,192,256]{2,1,0:T(8,128)(2,1)}), bf16[16,192,256]{2,1,0:T(8,128)(2,1)S(1)}, u32[]{:S(2)}, u32[]{:S(2)}) %all-to-all-start) | async-done | bytes 1572896 | tf_op jit(solution)/shard_map/all_to_all | solution.py:286
  49.4 8.2 %all-to-all-start.1 = ((bf16[8,2,960,128]{3,2,1,0:T(8,128)(2,1)}), bf16[8,2,960,128]{3,2,1,0:T(8,128)(2,1)}, u32[]{:S(2)}, u32[]{:S(2)}) async-start(bf16[8,2,960,128]{3,2,1,0:T(8,128)(2,1)} %maximum_bitcast_fusion), calls=%async_computation.1 | async-start | bytes 7864320 | tf_op jit(solution)/shard_map/all_to_all | solution.py:292
  57.6 0.1 copy.102
  57.8 0.1 reduce
  57.9 0.2 select_reduce_fusion
  58.1 1.7 copy.107.start_ref
  59.7 1.7 copy.108.prefix_ref
  61.4 0.2 compare_reduce_fusion
  61.7 0.1 copy.103
  61.7 0.1 reshape.241.flags
  61.9 56.3 %all-gather = bf16[16,2,2048]{2,1,0:T(2,128)(2,1)S(1)} all-gather(bf16[1,2,2048]{2,1,0:T(2,128)(2,1)S(1)} %bitcast.83), channel_id=1, replica_groups=mesh['kv'=2,'blk'=16] {'blk'}, dimensions={0}, use_global_device_ids=true | all-gather | bytes 139264 | tf_op jit(solution)/shard_map/all_gather | solution.py:319
  118.2 18.7 %all_gather.7 = bf16[2,32,1024]{2,0,1:T(2,128)(2,1)S(1)} all-gather(bf16[2,2,1024]{2,0,1:T(2,128)(2,1)S(1)} %copy.115), channel_id=1, replica_groups=mesh['kv'=2,'blk'=16] {'blk'}, dimensions={1}, use_global_device_ids=true | all-gather | bytes 139264 | tf_op jit(solution)/shard_map/all_gather | solution.py:320
  136.9 0.1 select_reduce_fusion.2
  137.2 0.1 convert_reduce_fusion.1.offsets
  137.3 0.2 convert_reduce_fusion
  137.4 0.1 select_reduce_fusion.3.order
  137.6 0.1 fusion.19
  137.7 0.2 select_reduce_fusion.4
  137.9 0.2 select_reduce_fusion.5
  138.2 0.2 fusion.9
  138.4 0.2 convolution_convert_fusion.1
  138.6 1.4 copy-done.2
  140.1 1.4 copy-done.3
  141.5 81.2 %head_attention.1 = (bf16[3072,256]{1,0:T(8,128)(2,1)S(1)}, f32[24,8,256]{2,1,0:T(8,128)S(1)}) custom-call(s32[48]{0:T(128)S(1)} %select_reduce_fusion.3.order, s32[5]{0:T(128)S(1)} %convert_reduce_fusion.1.offsets, s32[96]{0:T(128)S(1)} %reshape.241.flags, s32[24]{0:T(128)S(1)} %get-tuple-element.36.low, s32[24]{0:T(128)S(1)} %get-tuple-element.35.high, ...), custom_call_target="tpu_custom_call" | custom-call | tf_op jit(solution)/shard_map/head_attention/pallas_call | solution.py:210
  222.7 1.2 copy-done.4
  224.0 0.6 copy.111
  224.7 6.5 %all-to-all-start.3 = ((f32[16,2,192]{2,1,0:T(2,128)}), f32[16,2,192]{2,1,0:T(2,128)S(1)}, u32[]{:S(2)}, u32[]{:S(2)}) async-start(f32[16,2,192]{2,1,0:T(2,128)} %copy.111), calls=%async_computation.3 | async-start | bytes 65536 | tf_op jit(solution)/shard_map/all_to_all | solution.py:311
  231.2 6.6 %all-to-all-done.3 = f32[16,2,192]{2,1,0:T(2,128)S(1)} async-done(((f32[16,2,192]{2,1,0:T(2,128)}), f32[16,2,192]{2,1,0:T(2,128)S(1)}, u32[]{:S(2)}, u32[]{:S(2)}) %all-to-all-start.3) | async-done | bytes 24608 | tf_op jit(solution)/shard_map/all_to_all | solution.py:311
  237.8 3.7 all-to-all-start.2
  241.6 11.8 %copy.117 = bf16[2,16,128,1024]{2,3,1,0:T(8,128)(2,1)} copy(bf16[2,16,128,1024]{3,2,1,0:T(8,128)(2,1)} %param.25) | data formatting | bytes 16777216 | tf_op args[10]
  253.5 6.4 %broadcast_select_fusion = bf16[2,16,128,1024]{2,3,1,0:T(8,128)(2,1)S(1)} fusion(bf16[2,16,128,1024]{2,3,1,0:T(8,128)(2,1)} %copy.117, pred[16,128]{1,0:T(8,128)(4,1)S(1)} %fusion.25, bf16[2,16,1024]{2,1,0:T(8,128)(2,1)S(1)} %fusion.9), kind=kLoop, calls=%fused_computation | loop fusion | flops 4194304 | bytes 16844800 | tf_op jit(solution)/shard_map/jit(_where)/select_n | solution.py:338
  259.9 0.8 fusion.33
  260.7 2.4 copy-done.5
  263.1 1.3 fusion.34
  264.4 2.3 fusion.16
  266.6 0.4 convolution_convert_fusion.2
  267.1 0.7 copy.121
  267.9 0.1 copy.122
  268.0 0.3 convolution_convert_fusion.4
  268.3 0.6 dynamic-slice
  269.6 62.0 %all-reduce = bf16[32,8,2]{1,0,2:T(8,128)(2,1)S(1)} all-reduce(bf16[32,8,2]{1,0,2:T(8,128)(2,1)S(1)} %convolution_convert_fusion.4), channel_id=3, replica_groups=mesh['kv'=2,'blk'=16] {'blk'}, use_global_device_ids=true, to_apply=%region_14.15.clone | all-reduce | flops 512 | bytes 2048
  331.6 0.8 divide_convert_fusion
  332.4 0.1 copy.113
  332.6 3.0 reshape.242
  335.6 4.5 %reduce_sum.116 = f32[8,192,2,128]{3,2,1,0:T(2,128)S(1)} reduce(f32[2,8,192,2,128]{4,3,2,1,0:T(2,128)} %reshape.242, f32[]{:T(128)} %constant.119.clone.1), dimensions={0}, to_apply=%region_8.9 | reduce | flops 393216 | bytes 4718596 | tf_op jit(solution)/shard_map/reduce_sum | solution.py:313
  340.1 1.0 fusion.4
  341.2 0.8 copy.114
  342.0 0.6 reshape.238
  342.6 11.7 %convolution_convert_fusion = bf16[194,4608]{1,0:T(8,128)(2,1)} fusion(bf16[2048,4608]{1,0:T(8,128)(2,1)} %param.21, bf16[2,2048]{1,0:T(2,128)(2,1)S(1)} %reshape.240, bf16[192,2048]{1,0:T(8,128)(2,1)S(1)} %reshape.238), kind=kOutput, calls=%fused_computation.1 | convolution fusion | flops 3664110592 | bytes 21456896 | tf_op jit(solution)/shard_map/dot_general | solution.py:375
  354.3 11.7 %copy.125 = bf16[2,16,128,1024]{3,2,1,0:T(8,128)(2,1)} copy(bf16[2,16,128,1024]{2,3,1,0:T(8,128)(2,1)} %copy-done.5) | data formatting | bytes 16777216
  366.1 14.7 %reduce-scatter.6.cloned.1.call-done = bf16[194,2304]{1,0:T(8,128)(2,1)} async-done(((bf16[194,4608]{1,0:T(8,128)(2,1)}), bf16[194,2304]{1,0:T(8,128)(2,1)}) %reduce-scatter.6.cloned.1.call-update) | async-done | bytes 893968 | tf_op jit(solution)/shard_map/reduce_scatter | solution.py:377
  380.8 1.4 fusion
  382.2 4.9 %psum.7 = f32[194]{0:T(256)S(1)} all-reduce(f32[194]{0:T(256)S(1)} %fusion), channel_id=1, replica_groups=mesh['kv'=2,'blk'=16] {'kv'}, use_global_device_ids=true, to_apply=%region_17.18 | all-reduce | flops 194 | bytes 1552 | tf_op jit(solution)/shard_map/psum | solution.py:380
  387.2 1.6 fusion.3
  388.8 1.0 slice.31
  389.8 0.6 slice.32
  (64 shorter events, 0.8 us)
Async XLA Ops:
  7.2 13.6 %copy-start = (bf16[2,192,1024]{2,1,0:T(8,128)(2,1)S(1)}, bf16[2,192,1024]{2,1,0:T(8,128)(2,1)}, u32[]{:S(2)}) copy-start(bf16[2,192,1024]{2,1,0:T(8,128)(2,1)} %param.16) | copy-start | bytes 2359300
  10.1 39.3 %all-to-all-start = ((bf16[16,192,256]{2,1,0:T(8,128)(2,1)}), bf16[16,192,256]{2,1,0:T(8,128)(2,1)S(1)}, u32[]{:S(2)}, u32[]{:S(2)}) async-start(bf16[16,192,256]{2,1,0:T(8,128)(2,1)} %bitcast.70), calls=%async_computation | async-start | bytes 3145728 | tf_op jit(solution)/shard_map/all_to_all | solution.py:286
  23.2 34.4 %copy-start.12 = (s32[16]{0:T(128)S(1)}, s32[16]{0:T(128)}, u32[]{:S(2)}) copy-start(s32[16]{0:T(128)} %param.27) | copy-start | bytes 196
  23.2 34.7 %copy-start.13 = (s32[16]{0:T(128)S(1)}, s32[16]{0:T(128)}, u32[]{:S(2)}) copy-start(s32[16]{0:T(128)} %param.28) | copy-start | bytes 196
  49.4 89.2 %all-to-all-start.1 = ((bf16[8,2,960,128]{3,2,1,0:T(8,128)(2,1)}), bf16[8,2,960,128]{3,2,1,0:T(8,128)(2,1)}, u32[]{:S(2)}, u32[]{:S(2)}) async-start(bf16[8,2,960,128]{3,2,1,0:T(8,128)(2,1)} %maximum_bitcast_fusion), calls=%async_computation.1 | async-start | bytes 7864320 | tf_op jit(solution)/shard_map/all_to_all | solution.py:292
  57.6 4.3 %copy-start.10 = (bf16[2,2,1024]{2,1,0:T(2,128)(2,1)S(1)}, bf16[2,2,1024]{2,1,0:T(2,128)(2,1)}, u32[]{:S(2)}) copy-start(bf16[2,2,1024]{2,1,0:T(2,128)(2,1)} %param.19) | copy-start | bytes 24580
  57.6 4.3 %copy-start.9 = (bf16[2,2048]{1,0:T(2,128)(2,1)S(1)}, bf16[2,2048]{1,0:T(2,128)(2,1)}, u32[]{:S(2)}) copy-start(bf16[2,2048]{1,0:T(2,128)(2,1)} %param.18) | copy-start | bytes 24580
  57.6 79.4 %copy-start.14 = (s32[96]{0:T(128)S(1)}, s32[96]{0:T(128)}, u32[]{:S(2)}) copy-start(s32[96]{0:T(128)} %param.24) | copy-start | bytes 1156
  57.6 80.1 %copy-start.11 = (s32[256]{0:T(256)S(1)}, s32[256]{0:T(256)}, u32[]{:S(2)}) copy-start(s32[256]{0:T(256)} %param.26) | copy-start | bytes 3076
  57.6 80.3 %copy-start.15 = (s32[32]{0:T(128)S(1)}, s32[32]{0:T(128)}, u32[]{:S(2)}) copy-start(s32[32]{0:T(128)} %param.29) | copy-start | bytes 388
  138.6 1.4 copy-start.2
  140.1 1.4 copy-start.3
  222.7 1.2 copy-start.4
  224.7 13.1 %all-to-all-start.3 = ((f32[16,2,192]{2,1,0:T(2,128)}), f32[16,2,192]{2,1,0:T(2,128)S(1)}, u32[]{:S(2)}, u32[]{:S(2)}) async-start(f32[16,2,192]{2,1,0:T(2,128)} %copy.111), calls=%async_computation.3 | async-start | bytes 65536 | tf_op jit(solution)/shard_map/all_to_all | solution.py:311
  237.8 94.8 %all-to-all-start.2 = ((bf16[16,192,256]{2,1,0:T(8,128)(2,1)}), bf16[16,192,256]{2,1,0:T(8,128)(2,1)S(1)}, u32[]{:S(2)}, u32[]{:S(2)}) async-start(bf16[16,192,256]{2,1,0:T(8,128)(2,1)} %bitcast.66), calls=%async_computation.2 | async-start | bytes 3145728 | tf_op jit(solution)/shard_map/all_to_all | solution.py:310
  241.5 90.1 %reduce-scatter.4.cloned.1.call-start = ((), (), s32[]{:S(2)}) async-start(), calls=%async_computation.6 | async-start | bytes 139264 | tf_op jit(solution)/shard_map/reduce_scatter | solution.py:364
  259.9 3.2 copy-start.5
  264.4 3.9 copy-start.16
  267.8 113.0 %reduce-scatter.6.cloned.1.call-start = ((), (), s32[]{:S(2)}) async-start(), calls=%async_computation.7 | async-start | bytes 2764800 | tf_op jit(solution)/shard_map/reduce_scatter | solution.py:377
  354.3 32.9 %copy-start.6 = (bf16[192,2304]{1,0:T(8,128)(2,1)S(1)}, bf16[192,2304]{1,0:T(8,128)(2,1)}, u32[]{:S(2)}) copy-start(bf16[192,2304]{1,0:T(8,128)(2,1)} %param.17) | copy-start | bytes 2654212
  354.3 32.9 %copy-start.7 = (f32[2304]{0:T(1024)S(1)}, f32[2304]{0:T(1024)}, u32[]{:S(2)}) copy-start(f32[2304]{0:T(1024)} %param.22) | copy-start | bytes 27652
  354.3 32.9 %copy-start.8 = (bf16[2,2304]{1,0:T(2,128)(2,1)S(1)}, bf16[2,2304]{1,0:T(2,128)(2,1)}, u32[]{:S(2)}) copy-start(bf16[2,2304]{1,0:T(2,128)(2,1)} %param.20) | copy-start | bytes 27652
  354.3 36.1 %copy-start.1 = (bf16[2,192,1024]{2,1,0:T(8,128)(2,1)S(1)}, bf16[2,192,1024]{2,1,0:T(8,128)(2,1)}, u32[]{:S(2)}) copy-start(bf16[2,192,1024]{2,1,0:T(8,128)(2,1)} %param.16) | copy-start | bytes 2359300
Sparse Core Ops, SparseCore 0:
  267.9 56.3 reduce-scatter.3
  354.4 26.3 reduce-scatter.5

commit v2 on v1

v2 whole, which is shorter than its diff:
```python
import functools
import math

import jax
import jax.numpy as jnp
from jax import lax
from jax.experimental import pallas as pl
from jax.experimental.pallas import tpu as pltpu
from jax.sharding import PartitionSpec as P

D = 4608
QUERY_HEADS = 32
HEAD_SIZE = 128
PAGE_TOKENS = 128
PREFIX_LENGTH = 3072
SLOT_CAPACITY = 1024


soft_cap = 50.0
norm_eps = 1e-06


def token_tables(lengths, prefix_ids, token_ids):
    suffix_ends = jnp.cumsum(lengths)
    starts = suffix_ends - lengths
    inside = (
        (token_ids[:, None] >= starts[None, :]) & (token_ids[:, None] < suffix_ends[None, :])
    ).astype(jnp.int32)
    tok_start = jnp.sum(inside * starts[None, :], axis=1)
    tok_prefix = jnp.sum(inside * prefix_ids[None, :], axis=1)
    return (tok_start, tok_prefix)


def inverse_rows(table, wanted):
    hits = (table[None, :] == wanted[:, None]).astype(jnp.int32)
    places = jnp.arange(table.shape[0], dtype=jnp.int32)
    return jnp.sum(hits * places[None, :], axis=1)


PARTS = 2


def attention_kernel(
    places,
    offsets,
    flags,
    low,
    high,
    group_base,
    q_ref,
    start_ref,
    prefix_ref,
    kv_ref,
    numer_ref,
    denom_ref,
    acc,
    wacc,
    *,
    part,
    prefixes,
    local_pages,
    tok_rows,
    q_scale,
):
    page_len = PAGE_TOKENS
    tile_rows = q_ref.shape[1]
    section = local_pages * page_len + tok_rows
    tile = pl.program_id(0)
    q = q_ref[0]
    half = HEAD_SIZE
    rows_q = jnp.concatenate([q[:, :half], q[:, half:]], axis=0)
    row_prefix = prefix_ref[...]
    row_prefix = jnp.concatenate([row_prefix, row_prefix], axis=0)
    row_start = start_ref[...]
    row_start = jnp.concatenate([row_start, row_start], axis=0)
    inner = q_scale / soft_cap
    outer = soft_cap * math.log2(math.e)

    def weights_of(key_rows):
        logits = lax.dot_general(
            rows_q, key_rows, (((1,), (1,)), ((), ())), preferred_element_type=jnp.float32
        )
        return jnp.exp2(jnp.tanh(logits * inner) * outer)

    def folded(w):
        out = w[:, :half]
        for k in range(1, w.shape[1] // half):
            out = out + w[:, k * half : (k + 1) * half]
        return out

    def load(row, length):
        return kv_ref[pl.ds(pl.multiple_of(row, 64), length), :]

    row_id = (tile * PARTS + part) * tile_rows + lax.broadcasted_iota(
        jnp.int32, (tile_rows, 1), 0
    )
    row_id = jnp.concatenate([row_id, row_id], axis=0)
    acc[...] = jnp.zeros_like(acc)
    wacc[...] = jnp.zeros_like(wacc)
    span = 256

    def own(c, carry):
        first = group_base[0] + c * tok_rows
        row = (2 * c + 1) * section - span
        key_id = first + (tok_rows - span) + lax.broadcasted_iota(jnp.int32, (1, span), 1)
        seen = (key_id >= jnp.maximum(row_start, first)) & (key_id <= row_id)
        w = jnp.where(seen, weights_of(load(row, span)), 0.0)
        acc[...] += jnp.dot(
            w.astype(jnp.bfloat16), load(row + section, span), preferred_element_type=jnp.float32
        )
        wacc[...] += folded(w)
        return carry

    lax.fori_loop(low[tile], high[tile], own, 0)

    for p in range(prefixes):

        @pl.when(flags[tile * prefixes + p] != 0)
        def _():
            first = offsets[p]
            count = offsets[p + 1] - first
            keep = jnp.where(row_prefix == p, 1.0, 0.0)

            def step(width, c):
                rows = [places[first + c + k] for k in range(width)]
                key_rows = jnp.concatenate([load(r, page_len) for r in rows], axis=0)
                value_rows = jnp.concatenate([load(r + section, page_len) for r in rows], axis=0)
                w = weights_of(key_rows)
                num = jnp.dot(
                    w.astype(jnp.bfloat16), value_rows, preferred_element_type=jnp.float32
                )
                acc[...] += num * keep
                wacc[...] += folded(w) * keep

            def eight(c, carry):
                step(8, 8 * c)
                return carry

            lax.fori_loop(0, count // 8, eight, 0)
            for width in (4, 2, 1):

                @pl.when(count // width % 2 == 1)
                def _():
                    step(width, count // (2 * width) * (2 * width))

    numer_ref[0] = jnp.concatenate(
        [acc[:tile_rows, :], acc[tile_rows:, :]], axis=1
    ).astype(numer_ref.dtype)
    denom_ref[0] = lax.dot_general(
        jnp.ones((8, half), jnp.float32),
        wacc[...],
        (((1,), (1,)), ((), ())),
        preferred_element_type=jnp.float32,
        precision=lax.Precision.HIGHEST,
    )


def head_attention(part, q_part, kv_group, tok_start, tok_prefix, plan, base_token,
                   prefixes, local_pages, tok_rows, q_scale):
    tiles, tile_rows, width = q_part.shape
    sources = kv_group.shape[0]
    places, offsets = plan
    tile_start = tok_start.reshape(tiles, PARTS, tile_rows)[:, part]
    tile_prefix = tok_prefix.reshape(tiles, PARTS, tile_rows)[:, part]
    ids = jnp.arange(prefixes, dtype=jnp.int32)
    flags = jnp.any(tile_prefix[:, :, None] == ids[None, None, :], axis=1)
    flags = flags.astype(jnp.int32).reshape(-1)
    group_tokens = sources * tok_rows
    last = (jnp.arange(tiles, dtype=jnp.int32) * PARTS + part + 1) * tile_rows
    low = jnp.clip(tile_start[:, 0] - base_token, 0, group_tokens) // tok_rows
    high = (jnp.clip(last - base_token, 0, group_tokens) + tok_rows - 1) // tok_rows
    run = functools.partial(
        attention_kernel,
        part=part,
        prefixes=prefixes,
        local_pages=local_pages,
        tok_rows=tok_rows,
        q_scale=q_scale,
    )
    kv_rows = kv_group.reshape(-1, HEAD_SIZE)
    scores = 2 * tiles * tile_rows * kv_rows.shape[0] // 4
    return pl.pallas_call(
        run,
        out_shape=(
            jax.ShapeDtypeStruct((tiles, tile_rows, width), jnp.bfloat16),
            jax.ShapeDtypeStruct((tiles, 8, 2 * tile_rows), jnp.float32),
        ),
        grid_spec=pltpu.PrefetchScalarGridSpec(
            num_scalar_prefetch=6,
            grid=(tiles,),
            in_specs=[
                pl.BlockSpec((1, tile_rows, width), lambda i, *_: (i, 0, 0)),
                pl.BlockSpec((tile_rows, 1), lambda i, *_: (i, 0)),
                pl.BlockSpec((tile_rows, 1), lambda i, *_: (i, 0)),
                pl.BlockSpec(kv_rows.shape, lambda i, *_: (0, 0)),
            ],
            out_specs=[
                pl.BlockSpec((1, tile_rows, width), lambda i, *_: (i, 0, 0)),
                pl.BlockSpec((1, 8, 2 * tile_rows), lambda i, *_: (i, 0, 0)),
            ],
            scratch_shapes=[
                pltpu.VMEM((2 * tile_rows, HEAD_SIZE), jnp.float32),
                pltpu.VMEM((2 * tile_rows, HEAD_SIZE), jnp.float32),
            ],
        ),
        compiler_params=pltpu.CompilerParams(vmem_limit_bytes=32 * 1024 * 1024),
        cost_estimate=pl.CostEstimate(
            flops=16 * scores * HEAD_SIZE, bytes_accessed=8 * 1024 * 1024, transcendentals=2 * scores
        ),
        name="head_attention",
    )(places, offsets, flags, low, high, base_token[None], q_part,
      tile_start.reshape(-1, 1), tile_prefix.reshape(-1, 1), kv_rows)


def page_plan(owned, local_pages, tok_rows, prefixes):
    pages = owned.shape[0]
    place = jnp.arange(pages, dtype=jnp.int32)
    rank = owned * pages + place
    position = jnp.sum((rank[None, :] < rank[:, None]).astype(jnp.int32), axis=1)
    section = local_pages * PAGE_TOKENS + tok_rows
    row = place // local_pages * 2 * section + place % local_pages * PAGE_TOKENS
    places = jnp.sum((position[None, :] == place[:, None]).astype(jnp.int32) * row[None, :], axis=1)
    ids = jnp.arange(prefixes + 1, dtype=jnp.int32)
    offsets = jnp.sum((owned[None, :] < ids[:, None]).astype(jnp.int32), axis=1)
    return places, offsets


def two_halves(values):
    coarse = lax.reduce_precision(values, 8, 7)
    return [coarse.astype(jnp.bfloat16), (values - coarse).astype(jnp.bfloat16)]


def spread(block, axis="blk"):
    return lax.all_to_all(block, axis, 0, 0, tiled=True)


def finish(attention, residual, out_weight, post_gain):
    shares = lax.axis_size("kv")
    rows = attention.shape[0]
    projected = jnp.dot(attention, out_weight, preferred_element_type=jnp.float32)
    projected = projected.astype(jnp.bfloat16).reshape(rows, shares, -1).transpose(1, 0, 2)
    mine = jnp.sum(spread(projected, "kv").astype(jnp.float32), axis=0)
    mean_square = lax.psum(jnp.sum(mine * mine, axis=1), "kv") / D
    normed = mine * lax.rsqrt(mean_square + norm_eps)[:, None] * post_gain[None, :]
    return (residual.astype(jnp.float32) + normed).astype(jnp.bfloat16)


def body(
    suffix_query,
    suffix_key_value,
    suffix_resid,
    decode_query_rows,
    decode_key_value,
    decode_resid,
    out_weight,
    post_gain,
    prefix_page_store,
    prefix_table,
    decode_page_store,
    page_table,
    suffix_lengths,
    suffix_prefix,
    decode_ages,
):
    head_dim = HEAD_SIZE
    page_len = PAGE_TOKENS
    q_scale = (D // QUERY_HEADS) ** (-0.5)
    tok_rows = suffix_query.shape[0]
    q_heads = suffix_query.shape[1] // head_dim
    kv_heads = suffix_key_value.shape[2] // head_dim
    query_group_width = q_heads // kv_heads
    my_index = lax.axis_index("blk")
    blocks = lax.axis_size("blk")
    groups = blocks // kv_heads
    group = my_index // kv_heads
    pair = query_group_width * head_dim
    all_tokens = blocks * tok_rows
    part_rows = tok_rows // PARTS
    all_ids = jnp.arange(all_tokens, dtype=jnp.int32)
    tok_start, tok_prefix = token_tables(suffix_lengths, suffix_prefix, all_ids)
    pool_pages = prefix_table.shape[0]
    per_prefix = PREFIX_LENGTH // PAGE_TOKENS
    prefixes = pool_pages // per_prefix
    page_owner = (
        inverse_rows(prefix_table, jnp.arange(pool_pages, dtype=jnp.int32)) // per_prefix
    )
    local_pages = prefix_page_store.shape[1]
    group_pages = kv_heads * local_pages
    plan = page_plan(
        lax.dynamic_slice_in_dim(page_owner, group * group_pages, group_pages, 0),
        local_pages,
        tok_rows,
        prefixes,
    )
    q_heads_first = suffix_query.reshape(PARTS, part_rows, kv_heads, pair).transpose(0, 2, 1, 3)
    q_send = jnp.broadcast_to(
        q_heads_first[:, None], (PARTS, groups, kv_heads, part_rows, pair)
    ).reshape(PARTS, blocks, part_rows, pair)
    slot_rows = decode_query_rows.shape[0]
    decode_send = jnp.concatenate(
        [decode_query_rows, decode_key_value[0], decode_key_value[1]], axis=1
    )
    decode_width = decode_send.shape[1]
    decode_send = jnp.broadcast_to(
        decode_send.reshape(1, -1, pair), (blocks, slot_rows * decode_width // pair, pair)
    )
    first = spread(jnp.concatenate([q_send[0], decode_send], axis=1))
    kv_send = jnp.concatenate(
        [prefix_page_store.reshape(2, local_pages * page_len, -1), suffix_key_value], axis=1
    )
    kv_send = kv_send.reshape(2, -1, kv_heads, head_dim).transpose(2, 0, 1, 3)
    members = [[g * kv_heads + h for h in range(kv_heads)] for g in range(groups)]
    kv_group = lax.all_to_all(
        kv_send, "blk", 0, 0, tiled=True, axis_index_groups=members
    )
    q_parts = [first[:, :part_rows], spread(q_send[1])]
    decode_all = first[:, part_rows:].reshape(blocks * slot_rows, decode_width)
    all_dq = decode_all[:, : q_heads * head_dim]
    all_dkv = decode_all[:, q_heads * head_dim :].reshape(-1, 2, kv_heads * head_dim)
    all_dkv = all_dkv.transpose(1, 0, 2)
    slot_total = all_dq.shape[0]
    slot_pages = SLOT_CAPACITY // PAGE_TOKENS
    local_cache = decode_page_store.shape[1]
    page_ids = my_index * local_cache + jnp.arange(local_cache, dtype=jnp.int32)
    position = inverse_rows(page_table, page_ids)
    slot_of = position // slot_pages
    block_of = position % slot_pages
    slot_hot = slot_of[:, None] == jnp.arange(slot_total, dtype=jnp.int32)[None, :]
    page_age = jnp.sum(slot_hot.astype(jnp.int32) * decode_ages[None, :], axis=1)
    select = slot_hot.astype(jnp.bfloat16)
    new_rows = jnp.einsum(
        "ls,tsc->tlc", select, all_dkv, preferred_element_type=jnp.float32
    ).astype(jnp.bfloat16)
    write_here = (block_of == page_age // page_len)[:, None] & (
        jnp.arange(page_len, dtype=jnp.int32)[None, :] == (page_age % page_len)[:, None]
    )
    new_cache = jnp.where(write_here[None, :, :, None], new_rows[:, :, None, :], decode_page_store)
    page_queries = jnp.dot(select, all_dq, preferred_element_type=jnp.float32).astype(jnp.bfloat16)
    page_queries = page_queries.reshape(local_cache, kv_heads, query_group_width, head_dim)
    key_cache = new_cache[0].reshape(local_cache, page_len, kv_heads, head_dim)
    value_cache = new_cache[1].reshape(local_cache, page_len, kv_heads, head_dim)
    logits = (
        jnp.einsum("lhgd,lphd->lhgp", page_queries, key_cache, preferred_element_type=jnp.float32)
        * q_scale
    )
    capped = soft_cap * jnp.tanh(logits / soft_cap)
    places = block_of[:, None] * page_len + jnp.arange(page_len, dtype=jnp.int32)[None, :]
    seen_pos = places <= page_age[:, None]
    weights = jnp.where(seen_pos[:, None, None, :], jnp.exp(capped), 0.0)
    page_denom = jnp.sum(weights, axis=3)
    page_numer = jnp.einsum(
        "lhgp,lphd->lhgd",
        weights.astype(jnp.bfloat16),
        value_cache,
        preferred_element_type=jnp.float32,
    )
    slot_float = slot_hot.astype(jnp.float32)
    slot_numer = jnp.einsum(
        "ls,lhgd->shgd", slot_float, page_numer, precision=lax.Precision.HIGHEST
    )
    slot_denom = jnp.einsum("ls,lhg->shg", slot_float, page_denom, precision=lax.Precision.HIGHEST)
    slot_numer = slot_numer.astype(jnp.bfloat16).reshape(blocks, -1, pair)
    slot_denom = slot_denom.reshape(blocks, -1)
    decode_rows_sent = slot_numer.shape[1]
    decode_sums = slot_denom.shape[1]
    half_sums = query_group_width * part_rows
    hidden = []
    for part in range(PARTS):
        numer, denom = head_attention(
            part,
            q_parts[part],
            kv_group,
            tok_start,
            tok_prefix,
            plan,
            group * kv_heads * tok_rows,
            prefixes,
            local_pages,
            tok_rows,
            q_scale,
        )
        sums = two_halves(denom[:, 0, :])
        blocks_sent = [numer]
        if part == 0:
            sums = sums + two_halves(slot_denom)
            blocks_sent.append(slot_numer)
        sums = jnp.concatenate(sums, axis=1)
        sums = jnp.pad(sums, ((0, 0), (0, -sums.shape[1] % pair))).reshape(blocks, -1, pair)
        got = spread(jnp.concatenate(blocks_sent + [sums], axis=1))
        numer = got[:, :part_rows].reshape(
            groups, kv_heads, part_rows, query_group_width, head_dim
        )
        numer = jnp.sum(numer.astype(jnp.float32), axis=0)
        sums = got[:, -sums.shape[1] :].reshape(blocks, -1).astype(jnp.float32)
        denom = sums[:, :half_sums] + sums[:, half_sums : 2 * half_sums]
        denom = jnp.sum(
            denom.reshape(groups, kv_heads, query_group_width, part_rows), axis=0
        )
        attention = numer / denom.transpose(0, 2, 1)[..., None]
        attention = attention.astype(jnp.bfloat16).transpose(1, 0, 2, 3)
        attention = attention.reshape(part_rows, q_heads * head_dim)
        residual = suffix_resid[part * part_rows : (part + 1) * part_rows]
        if part == 0:
            mine_numer = got[:, part_rows : part_rows + decode_rows_sent].astype(jnp.float32)
            mine_numer = jnp.sum(mine_numer, axis=0).reshape(slot_rows, q_heads, head_dim)
            mine_denom = sums[:, 2 * half_sums : 2 * half_sums + 2 * decode_sums]
            mine_denom = jnp.sum(mine_denom.reshape(2 * blocks, slot_rows, q_heads), axis=0)
            decode_attn = (mine_numer / mine_denom[..., None]).astype(jnp.bfloat16)
            decode_attn = decode_attn.reshape(slot_rows, q_heads * head_dim)
            attention = jnp.concatenate([attention, decode_attn], axis=0)
            residual = jnp.concatenate([residual, decode_resid], axis=0)
        hidden.append(finish(attention, residual, out_weight, post_gain))
    suffix_hidden = jnp.concatenate([hidden[0][:part_rows], hidden[1]], axis=0)
    return (suffix_hidden, hidden[0][part_rows:], new_cache)


def solution(mesh):
    placed = (
        P("blk", "kv"),
        P(None, "blk", "kv"),
        P("blk", "kv"),
        P("blk", "kv"),
        P(None, "blk", "kv"),
        P("blk", "kv"),
        P("kv", None),
        P("kv"),
        P(None, "blk", None, "kv"),
        P(),
        P(None, "blk", None, "kv"),
        P(),
        P(),
        P(),
        P(),
    )
    return jax.shard_map(
        body,
        mesh=mesh,
        in_specs=placed,
        out_specs=(P("blk", "kv"), P("blk", "kv"), P(None, "blk", None, "kv")),
        check_vma=False,
    )
```

time: 401 us -> 283 us (0.71)
  blocking collectives: 142 us -> 4.93 us
  between operations: 15.2 us -> 1.35 us
  other arithmetic: 20 us -> 32.6 us
  starting transfers between devices: 25.8 us -> 35.9 us
  matrix products: 16.3 us -> 25.5 us
  local copies, waits for them, and re-layouts: 49.3 us -> 54.7 us
    all_gather x2 -> x0, blocking collectives: 75 us -> none  [the longest x1 56.3 us: body(): lax.all_gather(decode_query_rows, 'blk', axis=0, tiled=True)]
    unnamed x1 -> x0, blocking collectives: 62 us -> none
    all_to_all x1, waiting for transfers between devices: 0.01 us -> 21.9 us  [body(): lax.all_to_all(kv_send, 'blk', 0, 0, tiled=True, axis_index_groups=members)]
    reduce_scatter x2 -> x0, waiting for transfers between devices: 14.7 us -> none  [the longest x1 14.7 us: body(): lax.psum_scatter(projected.astype(jnp.bfloat16), 'kv', scatter_dimension=...]
    all_to_all x3 -> x6, starting transfers between devices: 17.5 us -> 31 us  [spread(): return lax.all_to_all(block, axis, 0, 0, tiled=True)]
    all_to_all x3 -> x6, waiting for transfers between devices: 32.8 us -> 23 us  [spread(): return lax.all_to_all(block, axis, 0, 0, tiled=True)]
    dot_general x1 -> x2, matrix products: 11.7 us -> 18.7 us  [finish(): jnp.dot(attention, out_weight, preferred_element_type=jnp.float32)]
    concatenate x0 -> x7, other arithmetic: none -> 5.32 us  [the longest x2 3.11 us: body(): got = spread(jnp.concatenate(blocks_sent + [sums], axis=1))]
  transfers between devices with their start and end apart: 6 -> 7, of which waited for: 3 -> 4; matrix products, arithmetic and copies ran while one was open for 12% -> 35% of each run, Pallas kernels for 0% -> 15%
where the time goes in v2:
time: 283 us; the launch traced here: 281 us
  Pallas kernels  81.7 us (29%)
  local copies, waits for them, and re-layouts  54.7 us (19%)
  waiting for transfers between devices  44.9 us (16%)
  starting transfers between devices  35.9 us (13%)
  other arithmetic  32.6 us (12%)
  matrix products  25.5 us (9%)
  blocking collectives  4.93 us (2%)
    pallas_call x2, Pallas kernels, head_attention(): pl.pallas_call(run, out_shape=(jax.ShapeDtypeStruct((tiles, tile_rows, wi...  81.7 us
    unnamed x39, local copies, waits for them, and re-layouts  32.9 us
    all_to_all x6, starting transfers between devices, spread(): return lax.all_to_all(block, axis, 0, 0, tiled=True)  31 us
    all_to_all x6, waiting for transfers between devices, spread(): return lax.all_to_all(block, axis, 0, 0, tiled=True)  23 us
    all_to_all x1, waiting for transfers between devices, body(): lax.all_to_all(kv_send, 'blk', 0, 0, tiled=True, axis_index_groups=members)  21.9 us
    dot_general x2, matrix products, finish(): jnp.dot(attention, out_weight, preferred_element_type=jnp.float32)  18.7 us
    select_n x1, other arithmetic, body(): jnp.where(write_here[None, :, :, None], new_rows[:, :, None, :], decode_p...  6.36 us
  transfers between devices with their start and end apart: 7, of which 4 were waited for; matrix products, arithmetic and copies ran while one was open for 35% of the time, Pallas kernels for 15%

profile of v2, /device:TPU:0, one launch (start us, length us, event | category | flops | bytes accessed | tf_op | source)
XLA Modules:
  0.0 281.5 jit_solution(15485218675259692315)
XLA Ops:
  0.7 1.4 copy.168
  2.3 1.0 broadcast_in_dim.47
  3.2 7.5 %all-to-all-start.4 = ((bf16[16,96,256]{2,1,0:T(8,128)(2,1)}), bf16[16,96,256]{2,1,0:T(8,128)(2,1)S(1)}, u32[]{:S(2)}, u32[]{:S(2)}) async-start(bf16[16,96,256]{2,1,0:T(8,128)(2,1)} %bitcast.25), calls=%async_computation.4 | async-start | bytes 1572864 | tf_op jit(solution)/shard_map/all_to_all | solution.py:234
  11.0 1.1 pad_maximum_fusion
  12.1 17.4 %all-to-all-done.4.q_ref = bf16[16,96,256]{2,1,0:T(8,128)(2,1)S(1)} async-done(((bf16[16,96,256]{2,1,0:T(8,128)(2,1)}), bf16[16,96,256]{2,1,0:T(8,128)(2,1)S(1)}, u32[]{:S(2)}, u32[]{:S(2)}) %all-to-all-start.4) | async-done | bytes 786464 | tf_op jit(solution)/shard_map/all_to_all | solution.py:234
  29.4 5.5 %all-to-all-start = ((bf16[16,128,256]{2,1,0:T(8,128)(2,1)}), bf16[16,128,256]{2,1,0:T(8,128)(2,1)}, u32[]{:S(2)}, u32[]{:S(2)}) async-start(bf16[16,128,256]{2,1,0:T(8,128)(2,1)} %pad_maximum_fusion), calls=%async_computation | async-start | bytes 2097152 | tf_op jit(solution)/shard_map/all_to_all | solution.py:234
  35.7 0.7 reshape_squeeze.24.start_ref
  36.4 0.7 reshape_squeeze.25.prefix_ref
  37.4 2.7 copy.169
  40.1 2.3 copy.134
  42.4 11.8 %copy.139 = bf16[2,16,128,1024]{2,3,1,0:T(8,128)(2,1)} copy(bf16[2,16,128,1024]{3,2,1,0:T(8,128)(2,1)} %param.25) | data formatting | bytes 16777216 | tf_op args[10]
  54.2 1.6 reshape_squeeze.26.start_ref
  55.8 1.6 reshape_squeeze.27.prefix_ref
  57.9 4.1 %maximum_bitcast_fusion = bf16[8,2,960,128]{3,2,1,0:T(8,128)(2,1)} fusion(bf16[2,192,8,128]{3,1,0,2:T(8,128)(2,1)S(1)} %copy_bitcast_fusion.1, bf16[2,768,8,128]{3,1,0,2:T(8,128)(2,1)} %copy.134), kind=kLoop, calls=%fused_computation.3 | loop fusion | flops 7864320 | bytes 7864320 | tf_op jit(solution)/shard_map/transpose | solution.py:311
  62.1 4.9 %all-to-all-start.1 = ((bf16[8,2,960,128]{3,2,1,0:T(8,128)(2,1)}), bf16[8,2,960,128]{3,2,1,0:T(8,128)(2,1)}, u32[]{:S(2)}, u32[]{:S(2)}) async-start(bf16[8,2,960,128]{3,2,1,0:T(8,128)(2,1)} %maximum_bitcast_fusion), calls=%async_computation.1 | async-start | bytes 7864320 | tf_op jit(solution)/shard_map/all_to_all | solution.py:313
  68.8 1.0 slice.143
  70.4 6.4 %broadcast_select_fusion = bf16[2,16,128,1024]{2,3,1,0:T(8,128)(2,1)S(1)} fusion(bf16[2,16,128,1024]{2,3,1,0:T(8,128)(2,1)} %copy.139, pred[16,128]{1,0:T(8,128)(4,1)S(1)} %fusion.41, bf16[2,16,1024]{2,1,0:T(8,128)(2,1)S(1)} %fusion.4), kind=kLoop, calls=%fused_computation | loop fusion | flops 4194304 | bytes 16844800 | tf_op jit(solution)/shard_map/jit(_where)/select_n | solution.py:337
  76.8 2.6 fusion.54
  79.4 1.8 copy-done.6
  81.2 1.3 fusion.56
  83.1 4.4 %fusion.14 = f32[16,8,2,128]{3,2,1,0:T(2,128)S(1)} fusion(bf16[16,128,8,128]{1,3,2,0:T(8,128)(2,1)} %bitcast.105, bf16[16,8,2,128]{3,2,1,0:T(2,128)(2,1)S(1)} %get-tuple-element.57), kind=kOutput, calls=%fused_computation.48 | convolution fusion | flops 8388608 | bytes 4390912 | tf_op jit(solution)/shard_map/lhgp,lphd->lhgd/dot_general | solution.py:351
  87.6 0.4 convolution_convert_fusion.3
  88.1 2.1 slice.142.q_ref
  90.2 21.9 %all-to-all-done.1 = bf16[8,2,960,128]{3,2,1,0:T(8,128)(2,1)} async-done(((bf16[8,2,960,128]{3,2,1,0:T(8,128)(2,1)}), bf16[8,2,960,128]{3,2,1,0:T(8,128)(2,1)}, u32[]{:S(2)}, u32[]{:S(2)}) %all-to-all-start.1) | async-done | bytes 3932192 | tf_op jit(solution)/shard_map/all_to_all | solution.py:313
  112.2 1.1 copy-done.3
  113.3 38.3 %head_attention.3 = (bf16[16,96,256]{2,1,0:T(8,128)(2,1)S(1)}, f32[16,8,192]{2,1,0:T(8,128)S(1)}) custom-call(s32[48]{0:T(128)S(1)} %select_reduce_fusion.3.places, s32[5]{0:T(128)S(1)} %convert_reduce_fusion.4.offsets, s32[64]{0:T(128)S(1)} %reshape.356.flags, s32[16]{0:T(128)S(1)} %add_select_fusion.low, s32[16]{0:T(128)S(1)} %and_select_fusion.high, ...), custom_call_target="tpu_custom_call" | custom-call | flops 24159191040 | bytes 8388608 | tf_op jit(solution)/shard_map/head_attention/pallas_call | solution.py:182
  151.6 0.9 copy-done.5
  152.6 2.1 pad_maximum_fusion.3
  154.7 4.5 %all-to-all-start.5 = ((bf16[16,98,256]{2,1,0:T(8,128)(2,1)}), bf16[16,98,256]{2,1,0:T(8,128)(2,1)}, u32[]{:S(2)}, u32[]{:S(2)}) async-start(bf16[16,98,256]{2,1,0:T(8,128)(2,1)} %pad_maximum_fusion.3), calls=%async_computation.5 | async-start | bytes 1703936 | tf_op jit(solution)/shard_map/all_to_all | solution.py:234
  159.2 1.1 copy-done.4
  160.4 43.4 %head_attention.2 = (bf16[16,96,256]{2,1,0:T(8,128)(2,1)S(1)}, f32[16,8,192]{2,1,0:T(8,128)S(1)}) custom-call(s32[48]{0:T(128)S(1)} %select_reduce_fusion.3.places, s32[5]{0:T(128)S(1)} %convert_reduce_fusion.4.offsets, s32[64]{0:T(128)S(1)} %reshape.352.flags, s32[16]{0:T(128)S(1)} %add_select_fusion.1.low, s32[16]{0:T(128)S(1)} %and_select_fusion.5.high, ...), custom_call_target="tpu_custom_call" | custom-call | flops 24159191040 | bytes 8388608 | tf_op jit(solution)/shard_map/head_attention/pallas_call | solution.py:182
  203.9 1.0 pad_maximum_fusion.1
  204.9 4.3 %all-to-all-start.2 = ((bf16[16,114,256]{2,1,0:T(8,128)(2,1)}), bf16[16,114,256]{2,1,0:T(8,128)(2,1)}, u32[]{:S(2)}, u32[]{:S(2)}) async-start(bf16[16,114,256]{2,1,0:T(8,128)(2,1)} %pad_maximum_fusion.1), calls=%async_computation.2 | async-start | bytes 1966080 | tf_op jit(solution)/shard_map/all_to_all | solution.py:234
  209.3 1.3 slice_convert_fusion
  210.6 0.8 reshape.358
  211.4 0.9 slice_convert_fusion.2
  212.4 1.6 reduce_sum.191
  214.2 0.5 fusion.5
  214.7 0.3 copy.156
  215.0 0.3 reshape.350
  215.3 9.5 %convolution_convert_fusion.1 = bf16[96,4608]{1,0:T(8,128)(2,1)S(1)} fusion(bf16[96,2048]{1,0:T(8,128)(2,1)S(1)} %reshape.350, bf16[2048,4608]{1,0:T(8,128)(2,1)} %param.21), kind=kOutput, calls=%fused_computation.2 | convolution fusion | flops 1812381696 | bytes 20152320 | tf_op jit(solution)/shard_map/dot_general | solution.py:240
  224.8 1.0 copy.192
  225.7 5.4 %all-to-all-done.2 = bf16[16,114,256]{2,1,0:T(8,128)(2,1)} async-done(((bf16[16,114,256]{2,1,0:T(8,128)(2,1)}), bf16[16,114,256]{2,1,0:T(8,128)(2,1)}, u32[]{:S(2)}, u32[]{:S(2)}) %all-to-all-start.2) | async-done | bytes 933920 | tf_op jit(solution)/shard_map/all_to_all | solution.py:234
  231.2 4.6 %all-to-all-start.6 = ((bf16[2,96,2304]{2,1,0:T(8,128)(2,1)}), bf16[2,96,2304]{2,1,0:T(8,128)(2,1)}, u32[]{:S(2)}, u32[]{:S(2)}) async-start(bf16[2,96,2304]{2,1,0:T(8,128)(2,1)} %bitcast.103), calls=%async_computation.6 | async-start | bytes 1769472 | tf_op jit(solution)/shard_map/all_to_all | solution.py:234
  235.8 0.9 slice_convert_fusion.3
  236.7 1.3 slice_convert_fusion.1
  238.0 0.8 reshape.354
  238.9 1.6 reduce_sum.184
  240.7 0.5 fusion.6
  241.2 0.3 copy.148
  241.5 0.3 reshape.344
  242.0 0.9 convert_reduce_fusion.2
  243.0 9.3 %convolution_convert_fusion = bf16[98,4608]{1,0:T(8,128)(2,1)S(1)} fusion(bf16[2048,4608]{1,0:T(8,128)(2,1)} %param.21, bf16[2,2048]{1,0:T(2,128)(2,1)S(1)} %fusion.30, bf16[96,2048]{1,0:T(8,128)(2,1)S(1)} %reshape.344), kind=kOutput, calls=%fused_computation.1 | convolution fusion | flops 1850942464 | bytes 20178944 | tf_op jit(solution)/shard_map/dot_general | solution.py:240
  252.3 0.3 reshape.347
  252.7 1.0 copy.191
  253.7 4.4 %all-to-all-start.3 = ((bf16[2,98,2304]{2,1,0:T(8,128)(2,1)}), bf16[2,98,2304]{2,1,0:T(8,128)(2,1)}, u32[]{:S(2)}, u32[]{:S(2)}) async-start(bf16[2,98,2304]{2,1,0:T(8,128)(2,1)} %bitcast.101), calls=%async_computation.3 | async-start | bytes 1916928 | tf_op jit(solution)/shard_map/all_to_all | solution.py:234
  258.1 11.8 %copy.158 = bf16[2,16,128,1024]{3,2,1,0:T(8,128)(2,1)} copy(bf16[2,16,128,1024]{2,3,1,0:T(8,128)(2,1)} %copy-done.6) | data formatting | bytes 16777216
  270.0 1.4 convert_reduce_fusion.1
  271.8 1.5 convert_reduce_fusion
  273.4 4.9 %all-reduce.2 = (f32[96]{0:T(128)S(1)}, f32[98]{0:T(128)S(1)}) all-reduce(f32[96]{0:T(128)S(1)} %multiply_reduce_fusion.1, f32[98]{0:T(128)S(1)} %multiply_reduce_fusion), channel_id=1, replica_groups=mesh['kv'=2,'blk'=16] {'kv'}, use_global_device_ids=true, to_apply=%region_23.24 | all-reduce | flops 194 | bytes 1552 | tf_op jit(solution)/shard_map/psum | solution.py:243
  278.4 0.2 add_convert_fusion
  278.7 0.6 slice.163
  279.3 1.2 add_convert_fusion.1
  280.5 1.0 pad_maximum_fusion.2
  (124 shorter events, 6.6 us)
Async XLA Ops:
  0.6 57.1 %copy-start = (bf16[2,192,1024]{2,1,0:T(8,128)(2,1)S(1)}, bf16[2,192,1024]{2,1,0:T(8,128)(2,1)}, u32[]{:S(2)}) copy-start(bf16[2,192,1024]{2,1,0:T(8,128)(2,1)} %param.16) | copy-start | bytes 2359300
  0.6 10.1 %copy-start.9 = (bf16[2,2,1024]{2,1,0:T(2,128)(2,1)S(1)}, bf16[2,2,1024]{2,1,0:T(2,128)(2,1)}, u32[]{:S(2)}) copy-start(bf16[2,2,1024]{2,1,0:T(2,128)(2,1)} %param.19) | copy-start | bytes 24580
  0.7 10.1 %copy-start.10 = (bf16[2,2048]{1,0:T(2,128)(2,1)S(1)}, bf16[2,2048]{1,0:T(2,128)(2,1)}, u32[]{:S(2)}) copy-start(bf16[2,2048]{1,0:T(2,128)(2,1)} %param.18) | copy-start | bytes 24580
  3.2 31.8 %copy-start.12 = (s32[16]{0:T(128)S(1)}, s32[16]{0:T(128)}, u32[]{:S(2)}) copy-start(s32[16]{0:T(128)} %param.27) | copy-start | bytes 196
  3.2 32.0 %copy-start.13 = (s32[16]{0:T(128)S(1)}, s32[16]{0:T(128)}, u32[]{:S(2)}) copy-start(s32[16]{0:T(128)} %param.28) | copy-start | bytes 196
  3.2 26.2 %all-to-all-start.4 = ((bf16[16,96,256]{2,1,0:T(8,128)(2,1)}), bf16[16,96,256]{2,1,0:T(8,128)(2,1)S(1)}, u32[]{:S(2)}, u32[]{:S(2)}) async-start(bf16[16,96,256]{2,1,0:T(8,128)(2,1)} %bitcast.25), calls=%async_computation.4 | async-start | bytes 1572864 | tf_op jit(solution)/shard_map/all_to_all | solution.py:234
  29.4 32.6 %all-to-all-start = ((bf16[16,128,256]{2,1,0:T(8,128)(2,1)}), bf16[16,128,256]{2,1,0:T(8,128)(2,1)}, u32[]{:S(2)}, u32[]{:S(2)}) async-start(bf16[16,128,256]{2,1,0:T(8,128)(2,1)} %pad_maximum_fusion), calls=%async_computation | async-start | bytes 2097152 | tf_op jit(solution)/shard_map/all_to_all | solution.py:234
  62.0 5.0 %copy-start.14 = (s32[96]{0:T(128)S(1)}, s32[96]{0:T(128)}, u32[]{:S(2)}) copy-start(s32[96]{0:T(128)} %param.24) | copy-start | bytes 1156
  62.1 6.1 %copy-start.11 = (s32[256]{0:T(256)S(1)}, s32[256]{0:T(256)}, u32[]{:S(2)}) copy-start(s32[256]{0:T(256)} %param.26) | copy-start | bytes 3076
  62.1 6.4 %copy-start.15 = (s32[32]{0:T(128)S(1)}, s32[32]{0:T(128)}, u32[]{:S(2)}) copy-start(s32[32]{0:T(128)} %param.29) | copy-start | bytes 388
  62.1 50.1 %all-to-all-start.1 = ((bf16[8,2,960,128]{3,2,1,0:T(8,128)(2,1)}), bf16[8,2,960,128]{3,2,1,0:T(8,128)(2,1)}, u32[]{:S(2)}, u32[]{:S(2)}) async-start(bf16[8,2,960,128]{3,2,1,0:T(8,128)(2,1)} %maximum_bitcast_fusion), calls=%async_computation.1 | async-start | bytes 7864320 | tf_op jit(solution)/shard_map/all_to_all | solution.py:313
  76.8 4.5 %copy-start.6 = (bf16[2,16,128,1024]{2,3,1,0:T(8,128)(2,1)}, bf16[2,16,128,1024]{2,3,1,0:T(8,128)(2,1)S(1)}, u32[]{:S(2)}) copy-start(bf16[2,16,128,1024]{2,3,1,0:T(8,128)(2,1)S(1)} %broadcast_select_fusion) | copy-start | bytes 25165828
  82.5 29.6 %copy-start.2 = (s32[1536,1]{1,0:T(8,128)S(1)}, s32[1536,1]{1,0:T(8,128)}, u32[]{:S(2)}) copy-start(s32[1536,1]{1,0:T(8,128)} %reshape_squeeze.26.start_ref) | copy-start | bytes 18436
  112.2 1.1 copy-start.3
  151.6 0.9 copy-start.5
  154.7 50.2 %all-to-all-start.5 = ((bf16[16,98,256]{2,1,0:T(8,128)(2,1)}), bf16[16,98,256]{2,1,0:T(8,128)(2,1)}, u32[]{:S(2)}, u32[]{:S(2)}) async-start(bf16[16,98,256]{2,1,0:T(8,128)(2,1)} %pad_maximum_fusion.3), calls=%async_computation.5 | async-start | bytes 1703936 | tf_op jit(solution)/shard_map/all_to_all | solution.py:234
  159.2 1.1 copy-start.4
  204.9 26.2 %all-to-all-start.2 = ((bf16[16,114,256]{2,1,0:T(8,128)(2,1)}), bf16[16,114,256]{2,1,0:T(8,128)(2,1)}, u32[]{:S(2)}, u32[]{:S(2)}) async-start(bf16[16,114,256]{2,1,0:T(8,128)(2,1)} %pad_maximum_fusion.1), calls=%async_computation.2 | async-start | bytes 1966080 | tf_op jit(solution)/shard_map/all_to_all | solution.py:234
  231.2 22.5 %all-to-all-start.6 = ((bf16[2,96,2304]{2,1,0:T(8,128)(2,1)}), bf16[2,96,2304]{2,1,0:T(8,128)(2,1)}, u32[]{:S(2)}, u32[]{:S(2)}) async-start(bf16[2,96,2304]{2,1,0:T(8,128)(2,1)} %bitcast.103), calls=%async_computation.6 | async-start | bytes 1769472 | tf_op jit(solution)/shard_map/all_to_all | solution.py:234
  253.7 18.1 %all-to-all-start.3 = ((bf16[2,98,2304]{2,1,0:T(8,128)(2,1)}), bf16[2,98,2304]{2,1,0:T(8,128)(2,1)}, u32[]{:S(2)}, u32[]{:S(2)}) async-start(bf16[2,98,2304]{2,1,0:T(8,128)(2,1)} %bitcast.101), calls=%async_computation.3 | async-start | bytes 1916928 | tf_op jit(solution)/shard_map/all_to_all | solution.py:234
  270.0 8.4 %slice-start = ((bf16[192,2304]{1,0:T(8,128)(2,1)}), bf16[96,2304]{1,0:T(8,128)(2,1)S(1)}, s32[]{:S(2)}) async-start(bf16[192,2304]{1,0:T(8,128)(2,1)} %param.17), calls=%async_computation.7 | async-start | bytes 884736 | tf_op jit(solution)/shard_map/slice | solution.py:402
  270.0 8.4 %copy-start.7 = (f32[2304]{0:T(1024)S(1)}, f32[2304]{0:T(1024)}, u32[]{:S(2)}) copy-start(f32[2304]{0:T(1024)} %param.22) | copy-start | bytes 27652
  270.0 8.4 %copy-start.8 = (bf16[2,2304]{1,0:T(2,128)(2,1)S(1)}, bf16[2,2304]{1,0:T(2,128)(2,1)}, u32[]{:S(2)}) copy-start(bf16[2,2304]{1,0:T(2,128)(2,1)} %param.20) | copy-start | bytes 27652
  271.8 9.7 %copy-start.1 = (bf16[2,192,1024]{2,1,0:T(8,128)(2,1)S(1)}, bf16[2,192,1024]{2,1,0:T(8,128)(2,1)}, u32[]{:S(2)}) copy-start(bf16[2,192,1024]{2,1,0:T(8,128)(2,1)} %param.16) | copy-start | bytes 2359300
